TPU v7x, 32 devices: a whole 2x2x4 slice. The times are simulated.
32 devices in a mesh: role: 4 (over y, x), section: 2 (over core), mp: 4 (over z).
Axes of the slice: x: 2, y: 2, z: 4, core: 2. Of those that a mesh axis runs over, the one named last changes fastest.
Arguments:
- states: bfloat16 [16, 64, 8192], P('role', None, 'mp'), may hold values from -6 to 6
- weights: bfloat16 [2, 8192, 8192], P('section', None, 'mp'), may hold values from -0.0625 to 0.0625
- head: bfloat16 [8192], P('mp'), may hold values from -0.0625 to 0.0625
- lengths: int32 [16], P('role'), may hold values from 1 to 64, as said below
- rewards: int32 [16], P('role'), may hold values from 0 to 1000
Outputs:
- weight_grads: bfloat16 [2, 8192, 8192], P('section', 'role', 'mp')
Inputs may be any that keep to these rules, and one draw needn't show every extreme that they name: `lengths`: at least one dialogue fills all 64 slots.
All inputs are finite; a program needn't handle non-finite values.
Results may differ from a plain program's by a relative error of at most 0.014.
Values may be sent and summed in bfloat16 or wider, within the bound.
No kernel may reach another device: no remote copies, remote signals or barrier semaphores. Data moves between devices by JAX's collectives and lax.ppermute only.
A program may use at most 384 MiB of HBM per device.

v0:
```python
import jax
import jax.numpy as jnp
from jax import lax
from jax.sharding import PartitionSpec as P

MB = 4


GAMMA = 0.97


def from_behind(block, axis, distance):
    devices = range(lax.axis_size(axis))
    route = [(i - distance, i) for i in devices if i - distance in devices]
    return lax.ppermute(block, axis, route)


def silu_slope(z):
    sig = jax.nn.sigmoid(z)
    return sig * (1.0 + z * (1.0 - sig))


def targets_of(lengths, rewards, span):
    places = jnp.arange(span, dtype=jnp.int32)[None, :]
    live = places < lengths[:, None]
    mask = live.astype(jnp.float32)
    power = jnp.where(live, lengths[:, None] - 1 - places, 0).astype(jnp.float32)
    target = (
        rewards.astype(jnp.float32)[:, None] / 1000.0 * jnp.power(jnp.float32(GAMMA), power) * mask
    )
    return (target.astype(jnp.bfloat16), mask)


def per_device(states, weights, head, lengths, rewards):
    dialogs, span, width = states.shape
    target, mask = targets_of(lengths, rewards, span)
    moved, moved_target, moved_mask = (
        lax.all_to_all(states, "role", split_axis=0, concat_axis=0, tiled=True),
        lax.all_to_all(target, "role", split_axis=0, concat_axis=0, tiled=True),
        lax.all_to_all(mask.astype(jnp.bfloat16), "role", split_axis=0, concat_axis=0, tiled=True),
    )
    block_rows = dialogs * span // MB
    goals = moved_target.astype(jnp.float32)
    row_masks = moved_mask.astype(jnp.float32)
    sections = lax.axis_size("section")
    section_index = lax.axis_index("section")
    turns = MB + sections - 1
    weight = weights[0]
    model_width = weight.shape[0]
    own_width = model_width // lax.axis_size("mp")
    head_f = head.astype(jnp.float32)
    is_first = section_index == 0
    is_last = section_index == sections - 1
    received = jnp.zeros((block_rows, width), jnp.bfloat16)
    kept_inputs = []
    kept_pre = []
    kept_value = []
    for turn in range(turns):
        own_rows = moved[turn] if turn < MB else jnp.zeros_like(received)
        inputs = jnp.where(is_first, own_rows, received)
        gathered = lax.all_gather(inputs, "mp", axis=1, tiled=True)
        pre = jnp.dot(gathered, weight, preferred_element_type=jnp.float32)
        output = (inputs.astype(jnp.float32) + jax.nn.silu(pre)).astype(jnp.bfloat16)
        value = lax.psum(jnp.dot(output, head, preferred_element_type=jnp.float32), "mp")
        kept_inputs.append(inputs)
        kept_pre.append(pre)
        kept_value.append(value)
        received = from_behind(output, "section", 1)
    accum = jnp.zeros((model_width, width), jnp.float32)
    incoming = jnp.zeros((block_rows, width), jnp.bfloat16)
    for turn in range(turns):
        forward_turn = turns - 1 - turn
        micro = forward_turn - section_index
        valid = ((micro >= 0) & (micro < MB)).astype(jnp.float32)
        head_micro = forward_turn - (sections - 1)
        if 0 <= head_micro < MB:
            error = (kept_value[forward_turn] - goals[head_micro]) * row_masks[head_micro]
        else:
            error = jnp.zeros((block_rows,), jnp.float32)
        from_head = error[:, None] * head_f[None, :]
        upstream = jnp.where(is_last, from_head, incoming.astype(jnp.float32)) * valid
        slope_grad = (upstream * silu_slope(kept_pre[forward_turn])).astype(jnp.bfloat16)

        def column_grad(piece, start, slope_grad=slope_grad):
            return lax.dot_general(
                piece, slope_grad, (((0,), (0,)), ((), ())), preferred_element_type=jnp.float32
            )

        accum = accum + column_grad(
            lax.all_gather(kept_inputs[forward_turn], "mp", axis=1, tiled=True), jnp.int32(0)
        )

        def back_term(start, count, slope_grad=slope_grad):
            return lax.dot_general(
                weight, slope_grad, (((1,), (1,)), ((), ())), preferred_element_type=jnp.float32
            )

        back = lax.psum_scatter(
            back_term(jnp.int32(0), own_width * lax.axis_size("mp")).astype(jnp.bfloat16),
            "mp",
            scatter_dimension=0,
            tiled=True,
        ).astype(jnp.float32)
        passed = (upstream + back.T).astype(jnp.bfloat16)
        incoming = from_behind(passed, "section", -1)
    summed = lax.psum_scatter(accum.astype(jnp.bfloat16), "role", scatter_dimension=0, tiled=True)
    return summed[None]


def solution(mesh):
    placed = (P("role", None, "mp"), P("section", None, "mp"), P("mp"), P("role"), P("role"))
    return jax.shard_map(
        per_device,
        mesh=mesh,
        in_specs=placed,
        out_specs=P("section", "role", "mp"),
        check_vma=False,
    )
```

profile of v0, /device:TPU:0, one launch (start us, length us, event | category | flops | bytes accessed | tf_op | source)
XLA Modules:
  0.0 890.8 jit_solution(11904396518484726938)
XLA Ops:
  6.5 5.2 all-to-all-start
  11.7 13.6 %all-to-all-done = bf16[4,64,2048]{2,1,0:T(8,128)(2,1)S(1)} async-done(((bf16[4,64,2048]{2,1,0:T(8,128)(2,1)}), bf16[4,64,2048]{2,1,0:T(8,128)(2,1)S(1)}, u32[]{:S(2)}, u32[]{:S(2)}) %all-to-all-start) | async-done | bytes 1048608 | tf_op jit(solution)/shard_map/all_to_all | solution.py:38
  26.1 28.4 %all-gather.15.cloned.1.call-done = bf16[1,64,8192]{2,1,0:T(8,128)(2,1)} async-done(((bf16[1,64,2048]{2,1,0:T(8,128)(2,1)}), bf16[1,64,8192]{2,1,0:T(8,128)(2,1)}) %all-gather.15.cloned.1.call-update) | async-done | bytes 1048592 | tf_op jit(solution)/shard_map/all_gather | solution.py:61
  54.5 17.6 %fusion.45 = (bf16[64,2048]{1,0:T(8,128)(2,1)S(1)}, f32[64,2048]{1,0:T(8,128)}) fusion(bf16[1,64,2048]{2,1,0:T(8,128)(2,1)} %slice_select_fusion, bf16[1,8192,2048]{2,1,0:T(8,128)(2,1)} %param.6, bf16[1,64,8192]{2,1,0:T(8,128)(2,1)} %all-gather.15.cloned.1.call-done), kind=kOutput, calls=%fused_computation.35 | convolution fusion | flops 2148401152 | bytes 35651584 | tf_op jit(solution)/shard_map/dot_general | solution.py:62
  72.0 1.6 collective-permute-start
  73.7 1.1 collective-permute-done
  75.6 27.8 %all-gather.7.cloned.1.call-done = bf16[64,8192]{1,0:T(8,128)(2,1)} async-done(((bf16[64,2048]{1,0:T(8,128)(2,1)}), bf16[64,8192]{1,0:T(8,128)(2,1)}) %all-gather.7.cloned.1.call-update) | async-done | bytes 1048592 | tf_op jit(solution)/shard_map/all_gather | solution.py:61
  103.4 16.8 %add_convert_fusion.4 = (bf16[64,2048]{1,0:T(8,128)(2,1)S(1)}, f32[64,2048]{1,0:T(8,128)S(1)}) fusion(bf16[64,2048]{1,0:T(8,128)(2,1)} %fusion.52, bf16[64,8192]{1,0:T(8,128)(2,1)} %all-gather.7.cloned.1.call-done, bf16[1,8192,2048]{2,1,0:T(8,128)(2,1)} %param.6), kind=kOutput, calls=%fused_computation.59 | convolution fusion | flops 2148401152 | bytes 35651584 | tf_op jit(solution)/shard_map/dot_general | solution.py:62
  120.2 1.6 collective-permute-start.1
  121.9 1.1 collective-permute-done.1
  124.0 27.6 %all-gather.9.cloned.1.call-done = bf16[64,8192]{1,0:T(8,128)(2,1)} async-done(((bf16[64,2048]{1,0:T(8,128)(2,1)}), bf16[64,8192]{1,0:T(8,128)(2,1)}) %all-gather.9.cloned.1.call-update) | async-done | bytes 1048592 | tf_op jit(solution)/shard_map/all_gather | solution.py:61
  151.6 16.8 %add_convert_fusion.3 = (bf16[64,2048]{1,0:T(8,128)(2,1)S(1)}, f32[64,2048]{1,0:T(8,128)S(1)}) fusion(bf16[64,2048]{1,0:T(8,128)(2,1)} %fusion.53, bf16[64,8192]{1,0:T(8,128)(2,1)} %all-gather.9.cloned.1.call-done, bf16[1,8192,2048]{2,1,0:T(8,128)(2,1)} %param.6), kind=kOutput, calls=%fused_computation.57 | convolution fusion | flops 2148401152 | bytes 35651584 | tf_op jit(solution)/shard_map/dot_general | solution.py:62
  168.4 1.6 collective-permute-start.2
  170.1 1.1 collective-permute-done.2
  172.0 27.9 %all-gather.11.cloned.1.call-done = bf16[64,8192]{1,0:T(8,128)(2,1)} async-done(((bf16[64,2048]{1,0:T(8,128)(2,1)}), bf16[64,8192]{1,0:T(8,128)(2,1)}) %all-gather.11.cloned.1.call-update) | async-done | bytes 1048592 | tf_op jit(solution)/shard_map/all_gather | solution.py:61
  199.8 16.8 %add_convert_fusion.2 = (bf16[64,2048]{1,0:T(8,128)(2,1)S(1)}, f32[64,2048]{1,0:T(8,128)S(1)}) fusion(bf16[64,2048]{1,0:T(8,128)(2,1)} %fusion.54, bf16[64,8192]{1,0:T(8,128)(2,1)} %all-gather.11.cloned.1.call-done, bf16[1,8192,2048]{2,1,0:T(8,128)(2,1)} %param.6), kind=kOutput, calls=%fused_computation.55 | convolution fusion | flops 2148401152 | bytes 35651584 | tf_op jit(solution)/shard_map/dot_general | solution.py:62
  216.6 1.6 collective-permute-start.3
  218.3 1.1 collective-permute-done.3
  220.8 3.7 all-to-all-start.2
  225.2 3.8 all-to-all-done.2
  229.0 3.2 all-to-all-start.1
  232.5 4.3 all-to-all-done.1
  237.3 10.7 %all-gather.13.cloned.1.call-done = bf16[64,8192]{1,0:T(8,128)(2,1)} async-done(((bf16[64,2048]{1,0:T(8,128)(2,1)}), bf16[64,8192]{1,0:T(8,128)(2,1)}) %all-gather.13.cloned.1.call-update) | async-done | bytes 1048592 | tf_op jit(solution)/shard_map/all_gather | solution.py:90
  248.0 13.9 %fusion.8 = f32[64,2048]{1,0:T(8,128)S(1)} fusion(bf16[64,8192]{1,0:T(8,128)(2,1)} %all-gather.13.cloned.1.call-done, bf16[1,8192,2048]{2,1,0:T(8,128)(2,1)} %param.6), kind=kOutput, calls=%fused_computation.9 | convolution fusion | flops 2147483648 | bytes 35127296 | tf_op jit(solution)/shard_map/dot_general | solution.py:62
  262.2 10.2 %all-reduce.1 = (f32[64]{0:T(128)S(1)}, f32[64]{0:T(128)S(1)}, f32[64]{0:T(128)S(1)}, f32[64]{0:T(128)S(1)}) all-reduce(f32[64]{0:T(128)S(1)} %convolution_bitcast_fusion.3, f32[64]{0:T(128)S(1)} %convolution_bitcast_fusion.2, f32[64]{0:T(128)S(1)} %convolution_bitcast_fusion.1, ...), channel_id=1, replica_groups=mesh['role'=4,'section'=2,'mp'=4] {'mp'}, use_global_device_ids=true, to_apply=%region_0.1 | all-reduce | flops 256 | bytes 2048 | tf_op jit(solution)/shard_map/psum | solution.py:64
  272.5 16.0 %fusion.39 = bf16[8192,64]{0,1:T(8,128)(2,1)} fusion(bf16[1,8192,2048]{2,1,0:T(8,128)(2,1)} %param.6, f32[64,2048]{1,0:T(8,128)S(1)} %fusion.8, f32[]{:T(128)S(6)} %convert_element_type.189, f32[2048]{0:T(1024)S(1)} %convert_element_type.188, f32[64]{0:T(128)S(1)} %get-tuple-element.12, pred[]{:T(512)S(6)} %eq.7), kind=kOutput, calls=%fused_computation.26 | convolution fusion | flops 2149580800 | bytes 35135748 | tf_op jit(solution)/shard_map/dot_general | solution.py:94
  288.5 25.4 %reduce-scatter.8.cloned.1.call-done = bf16[2048,64]{0,1:T(8,128)(2,1)} async-done(((bf16[8192,64]{0,1:T(8,128)(2,1)}), bf16[2048,64]{0,1:T(8,128)(2,1)}) %reduce-scatter.8.cloned.1.call-update) | async-done | bytes 262160 | tf_op jit(solution)/shard_map/reduce_scatter | solution.py:98
  315.0 1.3 collective-permute-start.4
  316.3 2.1 collective-permute-done.4
  318.5 15.9 %fusion.36 = bf16[8192,64]{0,1:T(8,128)(2,1)} fusion(bf16[1,8192,2048]{2,1,0:T(8,128)(2,1)} %param.6, f32[64,2048]{1,0:T(8,128)S(1)} %get-tuple-element.20, bf16[64,2048]{1,0:T(8,128)(2,1)S(1)} %collective-permute-done.4, f32[]{:T(128)S(6)} %convert_element_type.195, f32[64]{0:T(128)S(1)} %get-tuple-element.11, f32[2048]{0:T(1024)S(1)} %convert_element_type.188, ...), kind=kOutput, calls=%fused_computation.25 | convolution fusion | flops 2149711872 | bytes 35397892 | tf_op jit(solution)/shard_map/dot_general | solution.py:94
  334.5 25.9 %reduce-scatter.10.cloned.1.call-done = bf16[2048,64]{0,1:T(8,128)(2,1)} async-done(((bf16[8192,64]{0,1:T(8,128)(2,1)}), bf16[2048,64]{0,1:T(8,128)(2,1)}) %reduce-scatter.10.cloned.1.call-update) | async-done | bytes 262160 | tf_op jit(solution)/shard_map/reduce_scatter | solution.py:98
  360.4 1.1 fusion.48
  361.5 1.3 collective-permute-start.5
  362.8 2.1 collective-permute-done.5
  365.0 16.0 %fusion.33 = bf16[8192,64]{0,1:T(8,128)(2,1)} fusion(bf16[1,8192,2048]{2,1,0:T(8,128)(2,1)} %param.6, f32[64,2048]{1,0:T(8,128)S(1)} %get-tuple-element.18, bf16[64,2048]{1,0:T(8,128)(2,1)S(1)} %collective-permute-done.5, f32[]{:T(128)S(6)} %convert_element_type.201, f32[64]{0:T(128)S(1)} %get-tuple-element.10, f32[2048]{0:T(1024)S(1)} %convert_element_type.188, ...), kind=kOutput, calls=%fused_computation.24 | convolution fusion | flops 2149711872 | bytes 35397892 | tf_op jit(solution)/shard_map/dot_general | solution.py:94
  381.1 24.7 %fusion.69 = f32[8192,2048]{1,0:T(8,128)} fusion(bf16[64,8192]{1,0:T(8,128)(2,1)S(1)} %copy-done.3, f32[64,2048]{1,0:T(8,128)} %copy-done.5, f32[]{:T(128)S(6)} %convert_element_type.189, f32[2048]{0:T(1024)S(1)} %convert_element_type.188, f32[64]{0:T(128)S(1)} %get-tuple-element.12, pred[]{:T(512)S(6)} %eq.7), kind=kOutput, calls=%fused_computation.97 | convolution fusion | flops 2149056512 | bytes 68690184 | tf_op jit(solution)/shard_map/dot_general | solution.py:85
  405.8 1.1 reduce-scatter.12.cloned.1.call-done
  406.9 1.2 fusion.47
  408.2 1.5 collective-permute-start.6
  409.7 24.3 %fusion.70 = f32[8192,2048]{1,0:T(8,128)} fusion(bf16[64,8192]{1,0:T(8,128)(2,1)S(1)} %copy-done.2, f32[64,2048]{1,0:T(8,128)} %copy-done.4, bf16[64,2048]{1,0:T(8,128)(2,1)S(1)} %collective-permute-done.4, f32[]{:T(128)S(6)} %convert_element_type.195, f32[64]{0:T(128)S(1)} %get-tuple-element.11, f32[2048]{0:T(1024)S(1)} %convert_element_type.188, pred[]{:T(512)S(6)} %eq.7), kind=kOutput, calls=%fused_computation.98 | convolution fusion | flops 2149187584 | bytes 68952328 | tf_op jit(solution)/shard_map/dot_general | solution.py:85
  434.0 16.1 %fusion.30 = bf16[8192,64]{0,1:T(8,128)(2,1)} fusion(bf16[1,8192,2048]{2,1,0:T(8,128)(2,1)} %param.6, f32[64,2048]{1,0:T(8,128)S(1)} %get-tuple-element.16, bf16[64,2048]{1,0:T(8,128)(2,1)S(1)} %collective-permute-done.6, f32[]{:T(128)S(6)} %convert_element_type.207, f32[64]{0:T(128)S(1)} %get-tuple-element.9, f32[2048]{0:T(1024)S(1)} %convert_element_type.188, ...), kind=kOutput, calls=%fused_computation.23 | convolution fusion | flops 2149711872 | bytes 35397892 | tf_op jit(solution)/shard_map/dot_general | solution.py:94
  450.2 23.6 %fusion.71 = f32[8192,2048]{1,0:T(8,128)} fusion(bf16[64,8192]{1,0:T(8,128)(2,1)S(1)} %copy-done.1, f32[64,2048]{1,0:T(8,128)S(1)} %get-tuple-element.18, bf16[64,2048]{1,0:T(8,128)(2,1)S(1)} %copy-done.8, f32[]{:T(128)S(6)} %convert_element_type.201, f32[64]{0:T(128)S(1)} %get-tuple-element.10, f32[2048]{0:T(1024)S(1)} %convert_element_type.188, pred[]{:T(512)S(6)} %eq.7), kind=kOutput, calls=%fused_computation.99 | convolution fusion | flops 2149187584 | bytes 68952328 | tf_op jit(solution)/shard_map/dot_general | solution.py:85
  473.8 3.1 reduce-scatter.14.cloned.1.call-done
  476.9 1.2 fusion.46
  478.1 1.4 collective-permute-start.7
  479.5 24.2 %fusion.72 = f32[8192,2048]{1,0:T(8,128)} fusion(bf16[64,8192]{1,0:T(8,128)(2,1)S(1)} %copy-done, f32[64,2048]{1,0:T(8,128)S(1)} %get-tuple-element.16, bf16[64,2048]{1,0:T(8,128)(2,1)} %copy-done.9, f32[]{:T(128)S(6)} %convert_element_type.207, f32[64]{0:T(128)S(1)} %get-tuple-element.9, f32[2048]{0:T(1024)S(1)} %convert_element_type.188, pred[]{:T(512)S(6)} %eq.7), kind=kOutput, calls=%fused_computation.100 | convolution fusion | flops 2149187584 | bytes 68952328 | tf_op jit(solution)/shard_map/dot_general | solution.py:85
  503.8 91.5 %add_convert_fusion = bf16[8192,2048]{1,0:T(8,128)(2,1)} fusion(f32[8192,2048]{1,0:T(8,128)} %fusion.72, f32[8192,2048]{1,0:T(8,128)} %fusion.71, f32[8192,2048]{1,0:T(8,128)} %fusion.69, f32[8192,2048]{1,0:T(8,128)} %fusion.70, f32[64,2048]{1,0:T(8,128)S(1)} %copy-done.10, bf16[64,2048]{1,0:T(8,128)(2,1)S(1)} %collective-permute-done.7, ...), kind=kOutput, calls=%fused_computation | convolution fusion | flops 2232942592 | bytes 303833088 | tf_op jit(solution)/shard_map/dot_general | solution.py:85
  595.3 288.2 %reduce-scatter.16.cloned.1.call-done = bf16[2048,2048]{1,0:T(8,128)(2,1)} async-done(((bf16[8192,2048]{1,0:T(8,128)(2,1)}), bf16[2048,2048]{1,0:T(8,128)(2,1)}) %reduce-scatter.16.cloned.1.call-update) | async-done | bytes 8388624
  (72 shorter events, 7.9 us)
Async XLA Ops:
  6.5 18.8 %all-to-all-start = ((bf16[4,64,2048]{2,1,0:T(8,128)(2,1)}), bf16[4,64,2048]{2,1,0:T(8,128)(2,1)S(1)}, u32[]{:S(2)}, u32[]{:S(2)}) async-start(bf16[4,64,2048]{2,1,0:T(8,128)(2,1)} %param.5), calls=%async_computation | async-start | bytes 2097152 | tf_op jit(solution)/shard_map/all_to_all | solution.py:38
  11.7 42.8 %all-gather.15.cloned.1.call-start = ((), (), s32[]{:S(2)}) async-start(), calls=%async_computation.16 | async-start | bytes 1310720 | tf_op jit(solution)/shard_map/all_gather | solution.py:61
  26.1 77.4 %all-gather.7.cloned.1.call-start = ((), (), s32[]{:S(2)}) async-start(), calls=%async_computation.8 | async-start | bytes 1310720 | tf_op jit(solution)/shard_map/all_gather | solution.py:61
  72.0 2.7 collective-permute-start
  75.6 76.1 %all-gather.9.cloned.1.call-start = ((), (), s32[]{:S(2)}) async-start(), calls=%async_computation.9 | async-start | bytes 1310720 | tf_op jit(solution)/shard_map/all_gather | solution.py:61
  120.2 2.8 collective-permute-start.1
  123.7 96.4 %copy-start.13 = (s32[4]{0:T(128)S(1)}, s32[4]{0:T(128)}, u32[]{:S(2)}) copy-start(s32[4]{0:T(128)} %param.8) | copy-start | bytes 52
  123.8 100.7 %copy-start.14 = (s32[4]{0:T(128)S(1)}, s32[4]{0:T(128)}, u32[]{:S(2)}) copy-start(s32[4]{0:T(128)} %param.9) | copy-start | bytes 52
  123.8 108.6 %copy-start.12 = (bf16[2048]{0:T(1024)(128)(2,1)S(1)}, bf16[2048]{0:T(1024)(128)(2,1)}, u32[]{:S(2)}) copy-start(bf16[2048]{0:T(1024)(128)(2,1)} %param.7) | copy-start | bytes 12292
  123.8 76.1 %all-gather.11.cloned.1.call-start = ((), (), s32[]{:S(2)}) async-start(), calls=%async_computation.10 | async-start | bytes 1310720 | tf_op jit(solution)/shard_map/all_gather | solution.py:61
  168.4 2.8 collective-permute-start.2
  171.9 76.1 %all-gather.13.cloned.1.call-start = ((), (), s32[]{:S(2)}) async-start(), calls=%async_computation.11 | async-start | bytes 1310720 | tf_op jit(solution)/shard_map/all_gather | solution.py:90
  216.6 101.8 %copy-start.4 = (f32[64,2048]{1,0:T(8,128)}, f32[64,2048]{1,0:T(8,128)S(1)}, u32[]{:S(2)}) copy-start(f32[64,2048]{1,0:T(8,128)S(1)} %get-tuple-element.20) | copy-start | bytes 1572868
  216.6 2.8 collective-permute-start.3
  220.1 41.8 %copy-start.11 = (bf16[64,2048]{1,0:T(8,128)(2,1)S(1)}, bf16[64,2048]{1,0:T(8,128)(2,1)}, u32[]{:S(2)}) copy-start(bf16[64,2048]{1,0:T(8,128)(2,1)} %broadcast_select_fusion) | copy-start | bytes 786436
  220.8 8.2 all-to-all-start.2
  229.0 7.8 all-to-all-start.1
  232.2 81.8 %reduce-scatter.8.cloned.1.call-start = ((), (), s32[]{:S(2)}) async-start(), calls=%async_computation.12 | async-start | bytes 1310720 | tf_op jit(solution)/shard_map/reduce_scatter | solution.py:98
  261.9 72.4 %copy-start.5 = (f32[64,2048]{1,0:T(8,128)}, f32[64,2048]{1,0:T(8,128)S(1)}, u32[]{:S(2)}) copy-start(f32[64,2048]{1,0:T(8,128)S(1)} %fusion.8) | copy-start | bytes 1572868
  288.5 71.9 %reduce-scatter.10.cloned.1.call-start = ((), (), s32[]{:S(2)}) async-start(), calls=%async_computation.13 | async-start | bytes 1310720 | tf_op jit(solution)/shard_map/reduce_scatter | solution.py:98
  315.0 3.4 collective-permute-start.4
  334.4 46.7 %copy-start.3 = (bf16[64,8192]{1,0:T(8,128)(2,1)S(1)}, bf16[64,8192]{1,0:T(8,128)(2,1)}, u32[]{:S(2)}) copy-start(bf16[64,8192]{1,0:T(8,128)(2,1)} %all-gather.13.cloned.1.call-done) | copy-start | bytes 3145732
  334.4 72.5 %reduce-scatter.12.cloned.1.call-start = ((), (), s32[]{:S(2)}) async-start(), calls=%async_computation.14 | async-start | bytes 1310720 | tf_op jit(solution)/shard_map/reduce_scatter | solution.py:98
  361.5 3.4 collective-permute-start.5
  365.0 16.0 %copy-start.7 = (bf16[64,2048]{1,0:T(8,128)(2,1)}, bf16[64,2048]{1,0:T(8,128)(2,1)S(1)}, u32[]{:S(2)}) copy-start(bf16[64,2048]{1,0:T(8,128)(2,1)S(1)} %collective-permute-done.5) | copy-start | bytes 786436
  381.0 28.7 %copy-start.2 = (bf16[64,8192]{1,0:T(8,128)(2,1)S(1)}, bf16[64,8192]{1,0:T(8,128)(2,1)}, u32[]{:S(2)}) copy-start(bf16[64,8192]{1,0:T(8,128)(2,1)} %all-gather.11.cloned.1.call-done) | copy-start | bytes 3145732
  381.0 95.8 %reduce-scatter.14.cloned.1.call-start = ((), (), s32[]{:S(2)}) async-start(), calls=%async_computation.15 | async-start | bytes 1310720 | tf_op jit(solution)/shard_map/reduce_scatter | solution.py:98
  408.2 25.8 %collective-permute-start.6 = (bf16[64,2048]{1,0:T(8,128)(2,1)S(1)}, bf16[64,2048]{1,0:T(8,128)(2,1)S(1)}, u32[]{:S(2)}, u32[]{:S(2)}) collective-permute-start(bf16[64,2048]{1,0:T(8,128)(2,1)S(1)} %fusion.47), channel_id=1, source_target_pairs={{4,0},{5,1},{6,2},{7,3},{12,8},{13,9},{14,10},{15,11},{20,16},{21,... | collective-permute-start | bytes 786440 | tf_op jit(solution)/shard_map/ppermute | solution.py:15
  434.0 16.2 %copy-start.1 = (bf16[64,8192]{1,0:T(8,128)(2,1)S(1)}, bf16[64,8192]{1,0:T(8,128)(2,1)}, u32[]{:S(2)}) copy-start(bf16[64,8192]{1,0:T(8,128)(2,1)} %all-gather.9.cloned.1.call-done) | copy-start | bytes 3145732
  434.0 16.2 %copy-start.8 = (bf16[64,2048]{1,0:T(8,128)(2,1)S(1)}, bf16[64,2048]{1,0:T(8,128)(2,1)}, u32[]{:S(2)}) copy-start(bf16[64,2048]{1,0:T(8,128)(2,1)} %copy-done.7) | copy-start | bytes 786436
  434.0 16.1 %copy-start.9 = (bf16[64,2048]{1,0:T(8,128)(2,1)}, bf16[64,2048]{1,0:T(8,128)(2,1)S(1)}, u32[]{:S(2)}) copy-start(bf16[64,2048]{1,0:T(8,128)(2,1)S(1)} %collective-permute-done.6) | copy-start | bytes 786436
  450.1 29.4 %copy-start = (bf16[64,8192]{1,0:T(8,128)(2,1)S(1)}, bf16[64,8192]{1,0:T(8,128)(2,1)}, u32[]{:S(2)}) copy-start(bf16[64,8192]{1,0:T(8,128)(2,1)} %all-gather.7.cloned.1.call-done) | copy-start | bytes 3145732
  450.1 433.4 %reduce-scatter.16.cloned.1.call-start = ((), (), s32[]{:S(2)}) async-start(), calls=%async_computation.17 | async-start | bytes 41943040
  478.1 25.7 %copy-start.6 = (bf16[1,64,8192]{2,1,0:T(8,128)(2,1)S(1)}, bf16[1,64,8192]{2,1,0:T(8,128)(2,1)}, u32[]{:S(2)}) copy-start(bf16[1,64,8192]{2,1,0:T(8,128)(2,1)} %all-gather.15.cloned.1.call-done) | copy-start | bytes 3145732
  478.1 25.7 %copy-start.10 = (f32[64,2048]{1,0:T(8,128)S(1)}, f32[64,2048]{1,0:T(8,128)}, u32[]{:S(2)}) copy-start(f32[64,2048]{1,0:T(8,128)} %get-tuple-element.14) | copy-start | bytes 1572868
  478.1 25.6 %collective-permute-start.7 = (bf16[64,2048]{1,0:T(8,128)(2,1)S(1)}, bf16[64,2048]{1,0:T(8,128)(2,1)S(1)}, u32[]{:S(2)}, u32[]{:S(2)}) collective-permute-start(bf16[64,2048]{1,0:T(8,128)(2,1)S(1)} %fusion.46), channel_id=1, source_target_pairs={{4,0},{5,1},{6,2},{7,3},{12,8},{13,9},{14,10},{15,11},{20,16},{21,... | collective-permute-start | bytes 786440 | tf_op jit(solution)/shard_map/ppermute | solution.py:15
Sparse Core Ops, SparseCore 0:
  26.2 28.2 all-gather.14
  75.7 27.7 all-gather.6
  123.9 27.7 all-gather.8
  172.1 27.7 all-gather.10
  220.3 27.7 all-gather.12
  288.6 25.2 reduce-scatter.7
  334.5 25.8 reduce-scatter.9
  381.1 25.7 reduce-scatter.11
  450.2 26.5 reduce-scatter.13
  595.4 288.0 reduce-scatter.15
where the time goes:
time: 899 us; the launch traced here: 891 us
  waiting for transfers between devices  497 us (55%)
  matrix products  335 us (37%)
  starting transfers between devices  24.8 us (3%)
  between operations  14.3 us (2%)
  blocking collectives  10.2 us (1%)
  other arithmetic  9.68 us (1%)
    unnamed x11, waiting for transfers between devices  288 us
    dot_general x5, matrix products, column_grad(): lax.dot_general(piece, slope_grad, (((0,), (0,)), ((), ())), preferred_el...  188 us
    all_gather x4, waiting for transfers between devices, per_device(): gathered = lax.all_gather(inputs, 'mp', axis=1, tiled=True)  112 us
    dot_general x5, matrix products, per_device(): pre = jnp.dot(gathered, weight, preferred_element_type=jnp.float32)  81.8 us
    dot_general x4, matrix products, back_term(): lax.dot_general(weight, slope_grad, (((1,), (1,)), ((), ())), preferred_e...  64 us
    reduce_scatter x4, waiting for transfers between devices, per_device(): lax.psum_scatter(back_term(jnp.int32(0), own_width * lax.axis_size('mp'))...  55.5 us
  transfers between devices with their start and end apart: 21, of which 19 were waited for; matrix products, arithmetic and copies ran while one was open for 11% of the time, Pallas kernels for 0%

commit v1 on v0

v1 whole, which is shorter than its diff:
```python
import jax
import jax.numpy as jnp
from jax import lax
from jax.experimental import pallas as pl
from jax.experimental.pallas import tpu as pltpu
from jax.sharding import PartitionSpec as P

GAMMA = 0.97
AXES = ("role", "section", "mp")


def silu_slope(z):
    sig = jax.nn.sigmoid(z)
    return sig * (1.0 + z * (1.0 - sig))


def targets_of(lengths, rewards, span):
    places = jnp.arange(span, dtype=jnp.int32)[None, :]
    live = places < lengths[:, None]
    mask = live.astype(jnp.float32)
    power = jnp.where(live, lengths[:, None] - 1 - places, 0).astype(jnp.float32)
    target = (
        rewards.astype(jnp.float32)[:, None] / 1000.0 * jnp.power(jnp.float32(GAMMA), power) * mask
    )
    return target.astype(jnp.bfloat16), mask


def mm(a, b, dims):
    return lax.dot_general(a, b, (dims, ((), ())), preferred_element_type=jnp.float32)


COST = pl.CostEstimate(flops=1024, bytes_accessed=1024, transcendentals=0)
ANYWHERE = pl.BlockSpec(memory_space=pl.ANY)
IN_VMEM = pl.BlockSpec(memory_space=pltpu.VMEM)
PARAMS = pltpu.CompilerParams(vmem_limit_bytes=40 * 1024 * 1024)


def flip_a(part):
    return jnp.where((part == 1) | (part == 2), 2, 1)


def weight_index(which, part):
    if which == "own":
        return part
    if which == "a":
        return part ^ flip_a(part)
    if which == "b":
        return part ^ (3 - flip_a(part))
    if which == "c":
        return part ^ 3
    return jnp.int32(which)


def block_matmul(act, weight, which, core, back=False, add=None, out=jnp.float32, other=None):
    rows, depth = act.shape
    height, cols = weight.shape[1:]
    width = height if back else cols
    tile = min(512, width)
    tiles = width // tile

    def kernel(*refs):
        refs = list(refs)
        act_ref = refs.pop(0)
        other_ref = refs.pop(0) if other is not None else None
        add_ref = refs.pop(0) if add is not None else None
        weight_ref, out_ref, left, extra, held, sems, act_sems = refs

        @pl.when(lax.axis_index("section") == core)
        def _():
            j = weight_index(which, lax.axis_index("mp"))

            def fetch(i):
                cut = pl.ds(pl.multiple_of(i * tile, tile), tile)
                part = weight_ref.at[j, cut, :] if back else weight_ref.at[j, :, cut]
                return pltpu.make_async_copy(part, held.at[i], sems.at[i])

            loads = [pltpu.make_async_copy(act_ref, left, act_sems.at[0])]
            if other_ref is not None:
                loads.append(pltpu.make_async_copy(other_ref, extra, act_sems.at[1]))
            for load in loads:
                load.start()
            for i in range(tiles):
                fetch(i).start()
            for load in loads:
                load.wait()
            if other_ref is not None:
                left[...] = left[...] + extra[...]

            def step(i, carry):
                fetch(i).wait()
                cut = pl.ds(pl.multiple_of(i * tile, tile), tile)
                term = mm(left[...], held[i], ((1,), (1,) if back else (0,)))
                if add_ref is not None:
                    term = term + add_ref[:, cut]
                out_ref[:, cut] = term.astype(out)
                return carry

            lax.fori_loop(0, tiles, step, 0)

    args = [act] + ([other] if other is not None else [])
    specs = [ANYWHERE] * len(args)
    if add is not None:
        args.append(add)
        specs.append(IN_VMEM)
    return pl.pallas_call(
        kernel,
        out_shape=jax.ShapeDtypeStruct((rows, width), out),
        in_specs=specs + [ANYWHERE],
        out_specs=IN_VMEM,
        scratch_shapes=[
            pltpu.VMEM((rows, depth), act.dtype),
            pltpu.VMEM((rows, depth) if other is not None else (16, 128), act.dtype),
            pltpu.VMEM((tiles, tile, cols) if back else (tiles, height, tile), weight.dtype),
            pltpu.SemaphoreType.DMA((tiles,)),
            pltpu.SemaphoreType.DMA((2,)),
        ],
        compiler_params=PARAMS,
        cost_estimate=COST,
        name="back_block" if back else "forward_block",
    )(*args, weight)


def pick_blocks(blocks, core):
    count = 4

    def kernel(*refs):
        given, taken, sems = refs[:5], refs[5:9], refs[-1]

        @pl.when(lax.axis_index("section") == core)
        def _():
            part, role = lax.axis_index("mp"), lax.axis_index("role")
            inner = (part == 1) | (part == 2)
            for k in range(count):
                d = part ^ role ^ k
                slot = jnp.where(inner & ((d == 1) | (d == 2)), 3 - d, d)
                slot = jnp.where((slot == 3) & ~inner, 4, slot)
                for j in range(5):

                    @pl.when(slot == j)
                    def _():
                        pltpu.make_async_copy(given[j], taken[k], sems.at[k]).start()

            for k in range(count):
                pltpu.make_async_copy(given[0], taken[k], sems.at[k]).wait()

    return pl.pallas_call(
        kernel,
        out_shape=[jax.ShapeDtypeStruct(blocks[0].shape, blocks[0].dtype)] * count,
        in_specs=[ANYWHERE] * 5,
        out_specs=[IN_VMEM] * count,
        scratch_shapes=[pltpu.SemaphoreType.DMA((count,))],
        compiler_params=PARAMS,
        cost_estimate=COST,
        name="pick_blocks",
    )(*blocks)


def per_device(states, weights, head, lengths, rewards):
    dialogs, span, width = states.shape
    roles, sections, parts = (lax.axis_size(a) for a in AXES)
    role, section, part = (lax.axis_index(a) for a in AXES)
    rows = dialogs * span
    model = weights.shape[1]
    weight = weights[0].reshape(parts, width, width)
    own_cols = model // roles
    line = parts == 4 and roles == 4
    tie = lax.optimization_barrier

    def place(r, s, m):
        return (r * sections + s) * parts + m

    def along(block, hops, source, target):
        return lax.ppermute(
            block,
            AXES,
            [(place(r, source, i), place(r, target, j)) for r in range(roles) for i, j in hops],
        )

    def across(block, flip, source, target):
        return lax.ppermute(
            block,
            AXES,
            [
                (place(r, source, m), place(r ^ flip, target, m))
                for r in range(roles)
                for m in range(parts)
            ],
        )

    round_a = [(0, 2), (3, 1), (1, 0), (2, 3)]
    round_b = [(2, 0), (1, 3), (0, 1), (3, 2)]
    ends_in, ends_out = [(1, 0), (2, 3)], [(0, 1), (3, 2)]
    middle = [(1, 2), (2, 1)]
    swap = [(m, m) for m in range(parts)]
    near = [(i, i ^ 1) for i in range(4)]
    far = [(i, i ^ 2) for i in range(4)]

    def times(block, which, core, add=None, other=None):
        return block_matmul(block, weight, which, core, add=add, other=other)

    def forward_all(own, core):
        whole = lax.all_gather(own, "mp")
        blocks = [whole[j] for j in range(parts)]
        total = None
        for j in range(parts):
            total = times(blocks[j], j, core, total)
        return total, blocks

    def columns_of(blocks):
        if line:
            return pick_blocks(blocks, 0)
        full = jnp.concatenate(blocks, axis=1)
        return [
            lax.dynamic_slice_in_dim(full, (role ^ k) * own_cols, own_cols, 1) for k in range(roles)
        ]

    def sum_parts(v, core):
        if not line:
            return lax.psum(v, "mp")
        v = v + along(v, near, core, core)
        return v + along(v, far, core, core)

    target, mask = targets_of(lengths, rewards, span)
    goal = target.astype(jnp.float32).reshape(rows)
    keep = mask.reshape(rows)
    head_f = head.astype(jnp.float32)
    x = states.reshape(rows, width)

    if line:
        a = along(x, round_a, 0, 0)
        z0 = times(x, "own", 0)
        own, z0 = tie((x, z0))
        b = along(own, round_b, 0, 0)
        passed = along(a, ends_in, 0, 0)
        own, a = tie((own, a))
        mid = along(own, middle, 0, 0)
        z0 = times(a, "a", 0, z0)
        z0 = times(b, "b", 0, z0)
        z0 = times(mid, "c", 0, z0, passed)
        blocks = [x, a, b, mid, passed]
    else:
        z0, blocks = forward_all(x, 0)
    y1 = (x.astype(jnp.float32) + jax.nn.silu(z0)).astype(jnp.bfloat16)
    slope = silu_slope(z0)

    if line:
        a = along(y1, round_a, 0, 0)
        here = along(y1, swap, 0, 1)
        z1 = times(here, "own", 1)
        own, z1 = tie((y1, z1))
        x_cols = columns_of(blocks)
        x_got = [x_cols[0]] + [across(x_cols[k], k, 0, 0) for k in (1, 2)]
        b = along(own, round_b, 0, 0)
        a, b, x_got = tie((a, b, x_got))
        passed = along(a, ends_in, 0, 0)
        own, a = tie((own, a))
        mid = along(own, middle, 0, 0)
        x_got.append(across(x_cols[3], 3, 0, 0))
        z1 = times(along(a, swap, 0, 1), "a", 1, z1)
        z1 = times(along(b, swap, 0, 1), "b", 1, z1)
        ends = [(0, 0), (3, 3)]
        inside = [(1, 1), (2, 2)]
        z1 = times(along(mid, inside, 0, 1), "c", 1, z1, along(passed, ends, 0, 1))
        blocks = [y1, a, b, mid, passed]
    else:
        here = jnp.where(section == 1, along(y1, swap, 0, 1), y1)
        x_cols = columns_of(blocks)
        x_got = [x_cols[0]] + [across(x_cols[k], k, 0, 0) for k in range(1, roles)]
        z1, blocks = forward_all(here, 1)

    blocks, x_got = tie((blocks, x_got))
    y_cols = columns_of(blocks)
    grad = (head_f[None, :] * silu_slope(z1)).astype(jnp.bfloat16)
    y2 = (here.astype(jnp.float32) + jax.nn.silu(z1)).astype(jnp.bfloat16)
    value = jnp.sum(y2.astype(jnp.float32) * head_f[None, :], axis=1)

    value, y_cols = tie((value, y_cols))
    y_got = [y_cols[0]] + [across(y_cols[k], k, 0, 0) for k in range(1, roles)]
    value = along(value, swap, 1, 0)
    grad_0 = along(grad, swap, 1, 0)

    def term(which, grad, out=jnp.bfloat16):
        return block_matmul(grad, weight, which, 1, True, None, out)

    if line:
        c = term("c", grad)
        passed = along(c, ends_out, 1, 1)
        mid = along(c, middle, 1, 1)
        grad, value, c = tie((grad, value, c))
        b = term("b", grad)
        got_b = along(b, round_a, 1, 1)
        grad, b, grad_0 = tie((grad, b, grad_0))
        a = term("a", grad, jnp.float32)
        a = (a + passed.astype(jnp.float32)).astype(jnp.bfloat16)
        a, y_got[1], y_got[2] = tie((a, y_got[1], y_got[2]))
        got_a = along(a, round_b, 1, 1)
        grad, a = tie((grad, a))
        own = term("own", grad, jnp.float32)
        back = own + (mid.astype(jnp.float32) + got_b.astype(jnp.float32))
        back = (back + got_a.astype(jnp.float32)).astype(jnp.bfloat16)
    else:
        whole = jnp.stack([term(j, grad) for j in range(parts)])
        whole = jnp.where(section == 1, whole, jnp.zeros_like(whole))
        back = lax.psum_scatter(whole, "mp", scatter_dimension=0)

    value = sum_parts(value, 0)
    err = (value - goal) * keep
    dz1 = (err[:, None] * grad_0.astype(jnp.float32)).astype(jnp.bfloat16)
    dz1_got = [dz1] + [across(dz1, k, 0, 0) for k in range(1, roles)]
    back, y_got, dz1_got[1], dz1_got[2] = tie((back, y_got, dz1_got[1], dz1_got[2]))
    back = along(back, swap, 1, 0)

    dx1 = err[:, None] * (head_f[None, :] + back.astype(jnp.float32))
    dx1 = dx1.astype(jnp.bfloat16).astype(jnp.float32)
    dz0 = (dx1 * slope).astype(jnp.bfloat16)
    dz0_got = [dz0] + [across(dz0, k, 0, 0) for k in range(1, roles)]
    y_got = [along(t, swap, 0, 1) for t in y_got]
    dz1_got = [along(t, swap, 0, 1) for t in dz1_got]

    def weight_grad(lefts, rights):
        left, right = jnp.concatenate(lefts, axis=0), jnp.concatenate(rights, axis=0)
        return mm(left, right, ((0,), (0,))).astype(jnp.bfloat16)

    grads = lax.cond(
        section == 1,
        lambda x, y, p, q: weight_grad(y, q),
        lambda x, y, p, q: weight_grad(x, p),
        x_got,
        y_got,
        dz0_got,
        dz1_got,
    )
    return grads[None]


def solution(mesh):
    placed = (P("role", None, "mp"), P("section", None, "mp"), P("mp"), P("role"), P("role"))
    return jax.shard_map(
        per_device,
        mesh=mesh,
        in_specs=placed,
        out_specs=P("section", "role", "mp"),
        check_vma=False,
    )
```

time: 899 us -> 236 us (0.26)
  waiting for transfers between devices: 497 us -> 80.4 us
  matrix products: 335 us -> 11.7 us
  starting transfers between devices: 24.8 us -> 102 us
  Pallas kernels: 0 us -> 25.5 us
  between operations: 14.3 us -> 0.89 us
  blocking collectives: 10.2 us -> 0 us
    dot_general x18 -> x1, matrix products: 335 us -> 11.7 us  [mm(): lax.dot_general(a, b, (dims, ((), ())), preferred_element_type=jnp.float32)]
    unnamed x11 -> x0, waiting for transfers between devices: 288 us -> none
    all_gather x5 -> x0, waiting for transfers between devices: 122 us -> none  [the longest x4 112 us: per_device(): gathered = lax.all_gather(inputs, 'mp', axis=1, tiled=True)]
    ppermute x8 -> x42, starting transfers between devices: 12 us -> 102 us  [the longest x30 64.9 us: along(): lax.ppermute(block, AXES, [(place(r, source, i), place(r, target, j)) for...]
    ppermute x8 -> x42, waiting for transfers between devices: 8.76 us -> 80.4 us  [the longest x30 40.9 us: along(): lax.ppermute(block, AXES, [(place(r, source, i), place(r, target, j)) for...]
    reduce_scatter x4 -> x0, waiting for transfers between devices: 55.5 us -> none  [per_device(): lax.psum_scatter(back_term(jnp.int32(0), own_width * lax.axis_size('mp'))...]
    pallas_call x0 -> x14, Pallas kernels: none -> 25.5 us  [the longest x12 21.5 us: block_matmul(): pl.pallas_call(kernel, out_shape=jax.ShapeDtypeStruct((rows, width), out)...]
    all_to_all x3 -> x0, waiting for transfers between devices: 21.7 us -> none  [the longest x1 13.6 us: per_device(): lax.all_to_all(states, 'role', split_axis=0, concat_axis=0, tiled=True)]
  transfers between devices with their start and end apart: 21 -> 42, of which waited for: 19 -> 15; matrix products, arithmetic and copies ran while one was open for 11% -> 3% of each run, Pallas kernels for 0% -> 9%
where the time goes in v1:
time: 236 us; the launch traced here: 235 us
  starting transfers between devices  102 us (43%)
  waiting for transfers between devices  80.4 us (34%)
  Pallas kernels  25.5 us (11%)
  matrix products  11.7 us (5%)
  other arithmetic  7.97 us (3%)
  local copies, waits for them, and re-layouts  5.83 us (2%)
    ppermute x30, starting transfers between devices, along(): lax.ppermute(block, AXES, [(place(r, source, i), place(r, target, j)) for...  64.9 us
    ppermute x30, waiting for transfers between devices, along(): lax.ppermute(block, AXES, [(place(r, source, i), place(r, target, j)) for...  40.9 us
    ppermute x12, waiting for transfers between devices, across(): lax.ppermute(block, AXES, [(place(r, source, m), place(r ^ flip, target,...  39.5 us
    ppermute x12, starting transfers between devices, across(): lax.ppermute(block, AXES, [(place(r, source, m), place(r ^ flip, target,...  37.5 us
    pallas_call x12, Pallas kernels, block_matmul(): pl.pallas_call(kernel, out_shape=jax.ShapeDtypeStruct((rows, width), out)...  21.5 us
    dot_general x1, matrix products, mm(): lax.dot_general(a, b, (dims, ((), ())), preferred_element_type=jnp.float32)  11.7 us
    unnamed x34, local copies, waits for them, and re-layouts  5.51 us
  transfers between devices with their start and end apart: 42, of which 15 were waited for; matrix products, arithmetic and copies ran while one was open for 3% of the time, Pallas kernels for 9%

profile of v1, /device:TPU:0, one launch (start us, length us, event | category | flops | bytes accessed | tf_op | source)
XLA Modules:
  0.0 235.0 jit_solution(15194965847857828003)
XLA Ops:
  0.0 5.9 %collective-permute-start = (bf16[256,2048]{1,0:T(8,128)(2,1)}, bf16[256,2048]{1,0:T(8,128)(2,1)S(1)}, u32[]{:S(2)}, u32[]{:S(2)}) collective-permute-start(bf16[256,2048]{1,0:T(8,128)(2,1)} %bitcast.2.refs_0_), channel_id=1, source_target_pairs={{0,2},{3,1},{1,0},{2,3},{8,10},{11,9},{9,8},{10,11},{16,18},{19,17... | collective-permute-start | bytes 3145736 | tf_op jit(solution)/shard_map/ppermute | solution.py:173
  5.9 6.0 %forward_block.8.refs_1_ = f32[256,2048]{1,0:T(8,128)S(1)} custom-call(bf16[256,2048]{1,0:T(8,128)(2,1)} %bitcast.2.refs_0_, bf16[4,2048,2048]{2,1,0:T(8,128)(2,1)} %bitcast.7), custom_call_target="tpu_custom_call" | custom-call | flops 1024 | bytes 1024 | tf_op jit(solution)/shard_map/forward_block/pallas_call | solution.py:105
  12.0 1.9 collective-permute-start.3
  13.9 4.7 %collective-permute-done.refs_0_.refs_1_ = bf16[256,2048]{1,0:T(8,128)(2,1)S(1)} collective-permute-done((bf16[256,2048]{1,0:T(8,128)(2,1)}, bf16[256,2048]{1,0:T(8,128)(2,1)S(1)}, u32[]{:S(2)}, u32[]{:S(2)}) %collective-permute-start) | collective-permute-done | bytes 1048608 | tf_op jit(solution)/shard_map/ppermute | solution.py:173
  20.6 4.6 %forward_block.9.refs_1_ = f32[256,2048]{1,0:T(8,128)S(1)} custom-call(bf16[256,2048]{1,0:T(8,128)(2,1)S(1)} %collective-permute-done.refs_0_.refs_1_, f32[256,2048]{1,0:T(8,128)S(1)} %forward_block.8.refs_1_, bf16[4,2048,2048]{2,1,0:T(8,128)(2,1)} %bitcast.8), custom_call_target="tpu_custom_call" | custom-call | flops 1024 | bytes 1024 | tf_op jit(solution)/shard_map/forward_block/pallas_call | solution.py:105
  25.2 6.4 %collective-permute-done.3.refs_0_.refs_2_ = bf16[256,2048]{1,0:T(8,128)(2,1)S(1)} collective-permute-done((bf16[256,2048]{1,0:T(8,128)(2,1)}, bf16[256,2048]{1,0:T(8,128)(2,1)S(1)}, u32[]{:S(2)}, u32[]{:S(2)}) %collective-permute-start.3) | collective-permute-done | bytes 1048608 | tf_op jit(solution)/shard_map/ppermute | solution.py:173
  31.6 4.5 %forward_block.10.refs_2_ = f32[256,2048]{1,0:T(8,128)S(1)} custom-call(bf16[256,2048]{1,0:T(8,128)(2,1)S(1)} %collective-permute-done.3.refs_0_.refs_2_, f32[256,2048]{1,0:T(8,128)S(1)} %forward_block.9.refs_1_, bf16[4,2048,2048]{2,1,0:T(8,128)(2,1)} %bitcast.9), custom_call_target="tpu_custom_call" | custom-call | flops 1024 | bytes 1024 | tf_op jit(solution)/shard_map/forward_block/pallas_call | solution.py:105
  36.1 6.6 %collective-permute-done.2.refs_1_.refs_4_ = bf16[256,2048]{1,0:T(8,128)(2,1)S(1)} collective-permute-done((bf16[256,2048]{1,0:T(8,128)(2,1)S(1)}, bf16[256,2048]{1,0:T(8,128)(2,1)S(1)}, u32[]{:S(2)}, u32[]{:S(2)}) %collective-permute-start.2) | collective-permute-done | bytes 1048608 | tf_op jit(solution)/shard_map/ppermute | solution.py:173
  42.7 4.6 %forward_block.11 = f32[256,2048]{1,0:T(8,128)S(1)} custom-call(bf16[256,2048]{1,0:T(8,128)(2,1)S(1)} %collective-permute-done.1.refs_0_.refs_3_, bf16[256,2048]{1,0:T(8,128)(2,1)S(1)} %collective-permute-done.2.refs_1_.refs_4_, f32[256,2048]{1,0:T(8,128)S(1)} %forward_block.10.refs_2_, bf16[4,2048,2048]{2,1,0:T(8,128)(2,1)} %bitcast.10), custom_call_target="tpu_custom_call" | custom-call | flops 1024 | bytes 1024 | tf_op jit(solution)/shard_map/forward_block/pallas_call | solution.py:105
  47.3 1.9 add_convert_fusion.3.refs_0_
  49.3 1.4 collective-permute-start.4
  50.6 3.5 %collective-permute-start.5 = (bf16[256,2048]{1,0:T(8,128)(2,1)S(1)}, bf16[256,2048]{1,0:T(8,128)(2,1)S(1)}, u32[]{:S(2)}, u32[]{:S(2)}) collective-permute-start(bf16[256,2048]{1,0:T(8,128)(2,1)S(1)} %add_convert_fusion.3.refs_0_), channel_id=1, source_target_pairs={{0,2},{3,1},{1,0},{2,3},{8,10},{11,9},{9,8},{10,11},{16,18},{19,17... | collective-permute-start | bytes 3145736 | tf_op jit(solution)/shard_map/ppermute | solution.py:173
  54.2 2.3 pick_blocks.2
  56.4 3.5 %collective-permute-start.7 = (bf16[256,2048]{1,0:T(8,128)(2,1)S(1)}, bf16[256,2048]{1,0:T(8,128)(2,1)S(1)}, u32[]{:S(2)}, u32[]{:S(2)}) collective-permute-start(bf16[256,2048]{1,0:T(8,128)(2,1)S(1)} %get-tuple-element.113), channel_id=1, source_target_pairs={{0,8},{1,9},{2,10},{3,11},{8,0},{9,1},{10,2},{11,3},{16,24},{17,25... | collective-permute-start | bytes 3145736 | tf_op jit(solution)/shard_map/ppermute | solution.py:180
  59.9 3.6 %collective-permute-start.8 = (bf16[256,2048]{1,0:T(8,128)(2,1)S(1)}, bf16[256,2048]{1,0:T(8,128)(2,1)S(1)}, u32[]{:S(2)}, u32[]{:S(2)}) collective-permute-start(bf16[256,2048]{1,0:T(8,128)(2,1)S(1)} %get-tuple-element.114), channel_id=1, source_target_pairs={{0,16},{1,17},{2,18},{3,19},{8,24},{9,25},{10,26},{11,27},{16,0},{... | collective-permute-start | bytes 3145736 | tf_op jit(solution)/shard_map/ppermute | solution.py:180
  63.6 2.2 collective-permute-start.6
  65.9 1.4 collective-permute-done.5.refs_1_
  67.3 5.8 %collective-permute-done.7 = bf16[256,2048]{1,0:T(8,128)(2,1)S(1)} collective-permute-done((bf16[256,2048]{1,0:T(8,128)(2,1)S(1)}, bf16[256,2048]{1,0:T(8,128)(2,1)S(1)}, u32[]{:S(2)}, u32[]{:S(2)}) %collective-permute-start.7) | collective-permute-done | bytes 1048608 | tf_op jit(solution)/shard_map/ppermute | solution.py:180
  73.1 3.5 %collective-permute-done.8 = bf16[256,2048]{1,0:T(8,128)(2,1)S(1)} collective-permute-done((bf16[256,2048]{1,0:T(8,128)(2,1)S(1)}, bf16[256,2048]{1,0:T(8,128)(2,1)S(1)}, u32[]{:S(2)}, u32[]{:S(2)}) %collective-permute-start.8) | collective-permute-done | bytes 1048608 | tf_op jit(solution)/shard_map/ppermute | solution.py:180
  76.6 4.6 %collective-permute-done.6.refs_2_ = bf16[256,2048]{1,0:T(8,128)(2,1)S(1)} collective-permute-done((bf16[256,2048]{1,0:T(8,128)(2,1)S(1)}, bf16[256,2048]{1,0:T(8,128)(2,1)S(1)}, u32[]{:S(2)}, u32[]{:S(2)}) %collective-permute-start.6) | collective-permute-done | bytes 1048608 | tf_op jit(solution)/shard_map/ppermute | solution.py:173
  83.3 1.4 collective-permute-start.15
  86.7 11.9 %collective-permute-done.10.refs_4_ = bf16[256,2048]{1,0:T(8,128)(2,1)S(1)} collective-permute-done((bf16[256,2048]{1,0:T(8,128)(2,1)S(1)}, bf16[256,2048]{1,0:T(8,128)(2,1)S(1)}, u32[]{:S(2)}, u32[]{:S(2)}) %collective-permute-start.10) | collective-permute-done | bytes 1048608 | tf_op jit(solution)/shard_map/ppermute | solution.py:173
  100.0 2.6 %collective-permute-start.11 = (bf16[256,2048]{1,0:T(8,128)(2,1)S(1)}, bf16[256,2048]{1,0:T(8,128)(2,1)S(1)}, u32[]{:S(2)}, u32[]{:S(2)}) collective-permute-start(bf16[256,2048]{1,0:T(8,128)(2,1)S(1)} %get-tuple-element.122), channel_id=1, source_target_pairs={{0,24},{1,25},{2,26},{3,27},{8,16},{9,17},{10,18},{11,19},{16,8},{... | collective-permute-start | bytes 3145736 | tf_op jit(solution)/shard_map/ppermute | solution.py:180
  106.6 1.7 collective-permute-start.20
  108.2 9.4 %collective-permute-done.11 = bf16[256,2048]{1,0:T(8,128)(2,1)S(1)} collective-permute-done((bf16[256,2048]{1,0:T(8,128)(2,1)S(1)}, bf16[256,2048]{1,0:T(8,128)(2,1)S(1)}, u32[]{:S(2)}, u32[]{:S(2)}) %collective-permute-start.11) | collective-permute-done | bytes 1048608 | tf_op jit(solution)/shard_map/ppermute | solution.py:180
  117.6 1.8 pick_blocks.3
  121.5 2.3 collective-permute-start.21
  123.8 2.7 %collective-permute-start.22 = (bf16[256,2048]{1,0:T(8,128)(2,1)}, bf16[256,2048]{1,0:T(8,128)(2,1)}, u32[]{:S(2)}, u32[]{:S(2)}) collective-permute-start(bf16[256,2048]{1,0:T(8,128)(2,1)} %get-tuple-element.142), channel_id=1, source_target_pairs={{0,16},{1,17},{2,18},{3,19},{8,24},{9,25},{10,26},{11,27},{16,0},{... | collective-permute-start | bytes 3145736 | tf_op jit(solution)/shard_map/ppermute | solution.py:180
  128.0 1.7 collective-permute-done.16
  129.6 2.6 %collective-permute-start.17 = (f32[256]{0:T(256)S(1)}, f32[256]{0:T(256)S(1)}, u32[]{:S(2)}, u32[]{:S(2)}) collective-permute-start(f32[256]{0:T(256)S(1)} %collective-permute-done.16), channel_id=1, source_target_pairs={{0,1},{1,0},{2,3},{3,2},{8,9},{9,8},{10,11},{11,10},{16,17},{17,16... | collective-permute-start | bytes 3080 | tf_op jit(solution)/shard_map/ppermute | solution.py:173
  132.7 2.4 %collective-permute-done.17 = f32[256]{0:T(256)S(1)} collective-permute-done((f32[256]{0:T(256)S(1)}, f32[256]{0:T(256)S(1)}, u32[]{:S(2)}, u32[]{:S(2)}) %collective-permute-start.17) | collective-permute-done | bytes 1056 | tf_op jit(solution)/shard_map/ppermute | solution.py:173
  135.8 4.2 %collective-permute-start.26 = (bf16[256,2048]{1,0:T(8,128)(2,1)S(1)}, bf16[256,2048]{1,0:T(8,128)(2,1)S(1)}, u32[]{:S(2)}, u32[]{:S(2)}) collective-permute-start(bf16[256,2048]{1,0:T(8,128)(2,1)S(1)} %copy-done.3), channel_id=1, source_target_pairs={{0,24},{1,25},{2,26},{3,27},{8,16},{9,17},{10,18},{11,19},{16,8},{... | collective-permute-start | bytes 3145736 | tf_op jit(solution)/shard_map/ppermute | solution.py:180
  140.3 2.3 collective-permute-start.18
  142.5 1.6 add_convert_fusion.1
  146.7 1.5 multiply_convert_fusion.2
  148.2 2.2 collective-permute-start.28
  150.4 2.8 %collective-permute-start.27 = (bf16[256,2048]{1,0:T(8,128)(2,1)S(1)}, bf16[256,2048]{1,0:T(8,128)(2,1)}, u32[]{:S(2)}, u32[]{:S(2)}) collective-permute-start(bf16[256,2048]{1,0:T(8,128)(2,1)S(1)} %multiply_convert_fusion.2), channel_id=1, source_target_pairs={{0,8},{1,9},{2,10},{3,11},{8,0},{9,1},{10,2},{11,3},{16,24},{17,25... | collective-permute-start | bytes 3145736 | tf_op jit(solution)/shard_map/ppermute | solution.py:180
  153.4 4.3 %collective-permute-start.40 = (bf16[256,2048]{1,0:T(8,128)(2,1)S(1)}, bf16[256,2048]{1,0:T(8,128)(2,1)S(1)}, u32[]{:S(2)}, u32[]{:S(2)}) collective-permute-start(bf16[256,2048]{1,0:T(8,128)(2,1)S(1)} %multiply_convert_fusion.2), channel_id=1, source_target_pairs={{0,24},{1,25},{2,26},{3,27},{8,16},{9,17},{10,18},{11,19},{16,8},{... | collective-permute-start | bytes 3145736 | tf_op jit(solution)/shard_map/ppermute | solution.py:180
  157.7 18.6 %collective-permute-start.37 = (bf16[256,2048]{1,0:T(8,128)(2,1)S(1)}, bf16[256,2048]{1,0:T(8,128)(2,1)S(1)}, u32[]{:S(2)}, u32[]{:S(2)}) collective-permute-start(bf16[256,2048]{1,0:T(8,128)(2,1)S(1)} %multiply_convert_fusion.2), channel_id=1, source_target_pairs={{0,4},{1,5},{2,6},{3,7},{8,12},{9,13},{10,14},{11,15},{16,20},{17,... | collective-permute-start | bytes 3145736 | tf_op jit(solution)/shard_map/ppermute | solution.py:173
  179.5 1.9 collective-permute-start.41
  190.6 3.3 %collective-permute-start.32 = (bf16[256,2048]{1,0:T(8,128)(2,1)S(1)}, bf16[256,2048]{1,0:T(8,128)(2,1)}, u32[]{:S(2)}, u32[]{:S(2)}) collective-permute-start(bf16[256,2048]{1,0:T(8,128)(2,1)S(1)} %multiply_convert_fusion), channel_id=1, source_target_pairs={{0,24},{1,25},{2,26},{3,27},{8,16},{9,17},{10,18},{11,19},{16,8},{... | collective-permute-start | bytes 3145736 | tf_op jit(solution)/shard_map/ppermute | solution.py:180
  194.0 2.6 %collective-permute-start.31 = (bf16[256,2048]{1,0:T(8,128)(2,1)S(1)}, bf16[256,2048]{1,0:T(8,128)(2,1)}, u32[]{:S(2)}, u32[]{:S(2)}) collective-permute-start(bf16[256,2048]{1,0:T(8,128)(2,1)S(1)} %multiply_convert_fusion), channel_id=1, source_target_pairs={{0,16},{1,17},{2,18},{3,19},{8,24},{9,25},{10,26},{11,27},{16,0},{... | collective-permute-start | bytes 3145736 | tf_op jit(solution)/shard_map/ppermute | solution.py:180
  196.7 3.3 %collective-permute-start.30 = (bf16[256,2048]{1,0:T(8,128)(2,1)S(1)}, bf16[256,2048]{1,0:T(8,128)(2,1)}, u32[]{:S(2)}, u32[]{:S(2)}) collective-permute-start(bf16[256,2048]{1,0:T(8,128)(2,1)S(1)} %multiply_convert_fusion), channel_id=1, source_target_pairs={{0,8},{1,9},{2,10},{3,11},{8,0},{9,1},{10,2},{11,3},{16,24},{17,25... | collective-permute-start | bytes 3145736 | tf_op jit(solution)/shard_map/ppermute | solution.py:180
  200.0 8.4 %collective-permute-done.32 = bf16[256,2048]{1,0:T(8,128)(2,1)} collective-permute-done((bf16[256,2048]{1,0:T(8,128)(2,1)S(1)}, bf16[256,2048]{1,0:T(8,128)(2,1)}, u32[]{:S(2)}, u32[]{:S(2)}) %collective-permute-start.32) | collective-permute-done | bytes 1048608 | tf_op jit(solution)/shard_map/ppermute | solution.py:180
  208.4 11.1 %collective-permute-done.31 = bf16[256,2048]{1,0:T(8,128)(2,1)} collective-permute-done((bf16[256,2048]{1,0:T(8,128)(2,1)S(1)}, bf16[256,2048]{1,0:T(8,128)(2,1)}, u32[]{:S(2)}, u32[]{:S(2)}) %collective-permute-start.31) | collective-permute-done | bytes 1048608 | tf_op jit(solution)/shard_map/ppermute | solution.py:180
  219.6 12.0 %conditional.1 = (bf16[1,2048,2048]{2,1,0:T(8,128)(2,1)S(1)}) conditional(s32[]{:T(128)} %convert_element_type.83, (bf16[256,2048]{1,0:T(8,128)(2,1)}, bf16[256,2048]{1,0:T(8,128)(2,1)}, bf16[256,2048]{1,0:T(8,128)(2,1)}, bf16[256,2048]{1,0:T(8,128)(2,1)}, bf16[256,2048]{1,0:T(8,128)(2,1)S(1)}, /*index=5*/bf16[256,2048]{1,0:T(8,128)(2,1)}, ...), branch_computations={%region_1.2_spmd, %region_2.3_spmd} | conditional | flops 8627683328 | bytes 16777224 | solution.py:324
  219.6 11.7 %convert_bitcast_fusion = bf16[1,2048,2048]{2,1,0:T(8,128)(2,1)S(1)} fusion(bf16[256,2048]{1,0:T(8,128)(2,1)} %get-tuple-element.44, bf16[256,2048]{1,0:T(8,128)(2,1)} %get-tuple-element.43, bf16[256,2048]{1,0:T(8,128)(2,1)} %get-tuple-element.42, bf16[256,2048]{1,0:T(8,128)(2,1)} %get-tuple-element.41, bf16[256,2048]{1,0:T(8,128)(2,1)} %get-tuple-element.48, ...), kind=kOutput, calls=%fused_computation | convolution fusion | flops 8627683328 | bytes 16777216 | tf_op jit(solution)/shard_map/cond/branch_0_fun/dot_general | solution.py:29
  231.6 3.4 %copy-done.16 = bf16[1,2048,2048]{2,1,0:T(8,128)(2,1)} copy-done((bf16[1,2048,2048]{2,1,0:T(8,128)(2,1)}, bf16[1,2048,2048]{2,1,0:T(8,128)(2,1)S(1)}, u32[]{:S(2)}) %copy-start.16) | copy-done | bytes 8388632
  (103 shorter events, 31.3 us)
Async XLA Ops:
  0.0 18.6 %collective-permute-start = (bf16[256,2048]{1,0:T(8,128)(2,1)}, bf16[256,2048]{1,0:T(8,128)(2,1)S(1)}, u32[]{:S(2)}, u32[]{:S(2)}) collective-permute-start(bf16[256,2048]{1,0:T(8,128)(2,1)} %bitcast.2.refs_0_), channel_id=1, source_target_pairs={{0,2},{3,1},{1,0},{2,3},{8,10},{11,9},{9,8},{10,11},{16,18},{19,17... | collective-permute-start | bytes 3145736 | tf_op jit(solution)/shard_map/ppermute | solution.py:173
  12.0 19.6 %collective-permute-start.3 = (bf16[256,2048]{1,0:T(8,128)(2,1)}, bf16[256,2048]{1,0:T(8,128)(2,1)S(1)}, u32[]{:S(2)}, u32[]{:S(2)}) collective-permute-start(bf16[256,2048]{1,0:T(8,128)(2,1)} %bitcast.2.refs_0_), channel_id=1, source_target_pairs={{2,0},{1,3},{0,1},{3,2},{10,8},{9,11},{8,9},{11,10},{18,16},{17,19... | collective-permute-start | bytes 3145736 | tf_op jit(solution)/shard_map/ppermute | solution.py:173
  18.6 24.1 %collective-permute-start.2 = (bf16[256,2048]{1,0:T(8,128)(2,1)S(1)}, bf16[256,2048]{1,0:T(8,128)(2,1)S(1)}, u32[]{:S(2)}, u32[]{:S(2)}) collective-permute-start(bf16[256,2048]{1,0:T(8,128)(2,1)S(1)} %collective-permute-done.refs_0_.refs_1_), channel_id=1, source_target_pairs={{1,0},{2,3},{9,8},{10,11},{17,16},{18,19},{25,24},{26,27}} | collective-permute-start | bytes 3145736 | tf_op jit(solution)/shard_map/ppermute | solution.py:173
  19.9 22.8 %collective-permute-start.1 = (bf16[256,2048]{1,0:T(8,128)(2,1)}, bf16[256,2048]{1,0:T(8,128)(2,1)S(1)}, u32[]{:S(2)}, u32[]{:S(2)}) collective-permute-start(bf16[256,2048]{1,0:T(8,128)(2,1)} %bitcast.2.refs_0_), channel_id=1, source_target_pairs={{1,2},{2,1},{9,10},{10,9},{17,18},{18,17},{25,26},{26,25}} | collective-permute-start | bytes 3145736 | tf_op jit(solution)/shard_map/ppermute | solution.py:173
  49.3 14.3 %collective-permute-start.4 = (bf16[256,2048]{1,0:T(8,128)(2,1)S(1)}, bf16[256,2048]{1,0:T(8,128)(2,1)S(1)}, u32[]{:S(2)}, u32[]{:S(2)}) collective-permute-start(bf16[256,2048]{1,0:T(8,128)(2,1)S(1)} %add_convert_fusion.3.refs_0_), channel_id=1, source_target_pairs={{0,4},{1,5},{2,6},{3,7},{8,12},{9,13},{10,14},{11,15},{16,20},{17,... | collective-permute-start | bytes 3145736 | tf_op jit(solution)/shard_map/ppermute | solution.py:173
  50.6 16.7 %collective-permute-start.5 = (bf16[256,2048]{1,0:T(8,128)(2,1)S(1)}, bf16[256,2048]{1,0:T(8,128)(2,1)S(1)}, u32[]{:S(2)}, u32[]{:S(2)}) collective-permute-start(bf16[256,2048]{1,0:T(8,128)(2,1)S(1)} %add_convert_fusion.3.refs_0_), channel_id=1, source_target_pairs={{0,2},{3,1},{1,0},{2,3},{8,10},{11,9},{9,8},{10,11},{16,18},{19,17... | collective-permute-start | bytes 3145736 | tf_op jit(solution)/shard_map/ppermute | solution.py:173
  56.4 16.7 %collective-permute-start.7 = (bf16[256,2048]{1,0:T(8,128)(2,1)S(1)}, bf16[256,2048]{1,0:T(8,128)(2,1)S(1)}, u32[]{:S(2)}, u32[]{:S(2)}) collective-permute-start(bf16[256,2048]{1,0:T(8,128)(2,1)S(1)} %get-tuple-element.113), channel_id=1, source_target_pairs={{0,8},{1,9},{2,10},{3,11},{8,0},{9,1},{10,2},{11,3},{16,24},{17,25... | collective-permute-start | bytes 3145736 | tf_op jit(solution)/shard_map/ppermute | solution.py:180
  59.9 42.7 %copy-start.4 = (bf16[2048]{0:T(1024)(128)(2,1)S(1)}, bf16[2048]{0:T(1024)(128)(2,1)}, u32[]{:S(2)}) copy-start(bf16[2048]{0:T(1024)(128)(2,1)} %param.9) | copy-start | bytes 12292
  59.9 16.7 %collective-permute-start.8 = (bf16[256,2048]{1,0:T(8,128)(2,1)S(1)}, bf16[256,2048]{1,0:T(8,128)(2,1)S(1)}, u32[]{:S(2)}, u32[]{:S(2)}) collective-permute-start(bf16[256,2048]{1,0:T(8,128)(2,1)S(1)} %get-tuple-element.114), channel_id=1, source_target_pairs={{0,16},{1,17},{2,18},{3,19},{8,24},{9,25},{10,26},{11,27},{16,0},{... | collective-permute-start | bytes 3145736 | tf_op jit(solution)/shard_map/ppermute | solution.py:180
  63.6 17.6 %collective-permute-start.6 = (bf16[256,2048]{1,0:T(8,128)(2,1)S(1)}, bf16[256,2048]{1,0:T(8,128)(2,1)S(1)}, u32[]{:S(2)}, u32[]{:S(2)}) collective-permute-start(bf16[256,2048]{1,0:T(8,128)(2,1)S(1)} %add_convert_fusion.3.refs_0_), channel_id=1, source_target_pairs={{2,0},{1,3},{0,1},{3,2},{10,8},{9,11},{8,9},{11,10},{18,16},{17,19... | collective-permute-start | bytes 3145736 | tf_op jit(solution)/shard_map/ppermute | solution.py:173
  81.2 4.8 %collective-permute-start.9 = (bf16[256,2048]{1,0:T(8,128)(2,1)S(1)}, bf16[256,2048]{1,0:T(8,128)(2,1)S(1)}, u32[]{:S(2)}, u32[]{:S(2)}) collective-permute-start(bf16[256,2048]{1,0:T(8,128)(2,1)S(1)} %add_convert_fusion.3.refs_0_), channel_id=1, source_target_pairs={{1,2},{2,1},{9,10},{10,9},{17,18},{18,17},{25,26},{26,25}} | collective-permute-start | bytes 3145736 | tf_op jit(solution)/shard_map/ppermute | solution.py:173
  82.0 16.7 %collective-permute-start.10 = (bf16[256,2048]{1,0:T(8,128)(2,1)S(1)}, bf16[256,2048]{1,0:T(8,128)(2,1)S(1)}, u32[]{:S(2)}, u32[]{:S(2)}) collective-permute-start(bf16[256,2048]{1,0:T(8,128)(2,1)S(1)} %collective-permute-done.5.refs_1_), channel_id=1, source_target_pairs={{1,0},{2,3},{9,8},{10,11},{17,16},{18,19},{25,24},{26,27}} | collective-permute-start | bytes 3145736 | tf_op jit(solution)/shard_map/ppermute | solution.py:173
  83.3 19.4 %collective-permute-start.15 = (bf16[256,2048]{1,0:T(8,128)(2,1)S(1)}, bf16[256,2048]{1,0:T(8,128)(2,1)S(1)}, u32[]{:S(2)}, u32[]{:S(2)}) collective-permute-start(bf16[256,2048]{1,0:T(8,128)(2,1)S(1)} %collective-permute-done.5.refs_1_), channel_id=1, source_target_pairs={{0,4},{1,5},{2,6},{3,7},{8,12},{9,13},{10,14},{11,15},{16,20},{17,... | collective-permute-start | bytes 3145736 | tf_op jit(solution)/shard_map/ppermute | solution.py:173
  84.6 18.1 %collective-permute-start.14 = (bf16[256,2048]{1,0:T(8,128)(2,1)S(1)}, bf16[256,2048]{1,0:T(8,128)(2,1)S(1)}, u32[]{:S(2)}, u32[]{:S(2)}) collective-permute-start(bf16[256,2048]{1,0:T(8,128)(2,1)S(1)} %collective-permute-done.6.refs_2_), channel_id=1, source_target_pairs={{0,4},{1,5},{2,6},{3,7},{8,12},{9,13},{10,14},{11,15},{16,20},{17,... | collective-permute-start | bytes 3145736 | tf_op jit(solution)/shard_map/ppermute | solution.py:173
  86.0 16.8 %collective-permute-start.12 = (bf16[256,2048]{1,0:T(8,128)(2,1)S(1)}, bf16[256,2048]{1,0:T(8,128)(2,1)S(1)}, u32[]{:S(2)}, u32[]{:S(2)}) collective-permute-start(bf16[256,2048]{1,0:T(8,128)(2,1)S(1)} %collective-permute-done.9.refs_3_), channel_id=1, source_target_pairs={{1,5},{2,6},{9,13},{10,14},{17,21},{18,22},{25,29},{26,30}} | collective-permute-start | bytes 3145736 | tf_op jit(solution)/shard_map/ppermute | solution.py:173
  98.7 4.2 %collective-permute-start.13 = (bf16[256,2048]{1,0:T(8,128)(2,1)S(1)}, bf16[256,2048]{1,0:T(8,128)(2,1)S(1)}, u32[]{:S(2)}, u32[]{:S(2)}) collective-permute-start(bf16[256,2048]{1,0:T(8,128)(2,1)S(1)} %collective-permute-done.10.refs_4_), channel_id=1, source_target_pairs={{0,4},{3,7},{8,12},{11,15},{16,20},{19,23},{24,28},{27,31}} | collective-permute-start | bytes 3145736 | tf_op jit(solution)/shard_map/ppermute | solution.py:173
  100.0 17.6 %collective-permute-start.11 = (bf16[256,2048]{1,0:T(8,128)(2,1)S(1)}, bf16[256,2048]{1,0:T(8,128)(2,1)S(1)}, u32[]{:S(2)}, u32[]{:S(2)}) collective-permute-start(bf16[256,2048]{1,0:T(8,128)(2,1)S(1)} %get-tuple-element.122), channel_id=1, source_target_pairs={{0,24},{1,25},{2,26},{3,27},{8,16},{9,17},{10,18},{11,19},{16,8},{... | collective-permute-start | bytes 3145736 | tf_op jit(solution)/shard_map/ppermute | solution.py:180
  104.2 31.6 %collective-permute-start.19 = (bf16[256,2048]{1,0:T(8,128)(2,1)S(1)}, bf16[256,2048]{1,0:T(8,128)(2,1)}, u32[]{:S(2)}, u32[]{:S(2)}) collective-permute-start(bf16[256,2048]{1,0:T(8,128)(2,1)S(1)} %get-tuple-element.144.refs_0_), channel_id=1, source_target_pairs={{4,0},{5,1},{6,2},{7,3},{12,8},{13,9},{14,10},{15,11},{20,16},{21,... | collective-permute-start | bytes 3145736 | tf_op jit(solution)/shard_map/ppermute | solution.py:173
  106.6 33.7 %collective-permute-start.20 = (bf16[256,2048]{1,0:T(8,128)(2,1)}, bf16[256,2048]{1,0:T(8,128)(2,1)}, u32[]{:S(2)}, u32[]{:S(2)}) collective-permute-start(bf16[256,2048]{1,0:T(8,128)(2,1)} %back_block.4), channel_id=1, source_target_pairs={{4,5},{7,6},{12,13},{15,14},{20,21},{23,22},{28,29},{31,30}} | collective-permute-start | bytes 3145736 | tf_op jit(solution)/shard_map/ppermute | solution.py:173
  108.2 24.0 %copy-start.15 = (s32[4]{0:T(128)S(1)}, s32[4]{0:T(128)}, u32[]{:S(2)}) copy-start(s32[4]{0:T(128)} %param.11) | copy-start | bytes 52
  121.5 22.6 %collective-permute-start.21 = (bf16[256,2048]{1,0:T(8,128)(2,1)}, bf16[256,2048]{1,0:T(8,128)(2,1)}, u32[]{:S(2)}, u32[]{:S(2)}) collective-permute-start(bf16[256,2048]{1,0:T(8,128)(2,1)} %get-tuple-element.141), channel_id=1, source_target_pairs={{0,8},{1,9},{2,10},{3,11},{8,0},{9,1},{10,2},{11,3},{16,24},{17,25... | collective-permute-start | bytes 3145736 | tf_op jit(solution)/shard_map/ppermute | solution.py:180
  123.8 21.0 %collective-permute-start.22 = (bf16[256,2048]{1,0:T(8,128)(2,1)}, bf16[256,2048]{1,0:T(8,128)(2,1)}, u32[]{:S(2)}, u32[]{:S(2)}) collective-permute-start(bf16[256,2048]{1,0:T(8,128)(2,1)} %get-tuple-element.142), channel_id=1, source_target_pairs={{0,16},{1,17},{2,18},{3,19},{8,24},{9,25},{10,26},{11,27},{16,0},{... | collective-permute-start | bytes 3145736 | tf_op jit(solution)/shard_map/ppermute | solution.py:180
  126.6 3.0 %collective-permute-start.16 = (f32[256]{0:T(256)S(1)}, f32[256]{0:T(256)S(1)}, u32[]{:S(2)}, u32[]{:S(2)}) collective-permute-start(f32[256]{0:T(256)S(1)} %get-tuple-element.137), channel_id=1, source_target_pairs={{4,0},{5,1},{6,2},{7,3},{12,8},{13,9},{14,10},{15,11},{20,16},{21,... | collective-permute-start | bytes 3080 | tf_op jit(solution)/shard_map/ppermute | solution.py:173
  129.6 5.5 %collective-permute-start.17 = (f32[256]{0:T(256)S(1)}, f32[256]{0:T(256)S(1)}, u32[]{:S(2)}, u32[]{:S(2)}) collective-permute-start(f32[256]{0:T(256)S(1)} %collective-permute-done.16), channel_id=1, source_target_pairs={{0,1},{1,0},{2,3},{3,2},{8,9},{9,8},{10,11},{11,10},{16,17},{17,16... | collective-permute-start | bytes 3080 | tf_op jit(solution)/shard_map/ppermute | solution.py:173
  135.1 15.3 %collective-permute-start.23 = (bf16[256,2048]{1,0:T(8,128)(2,1)}, bf16[256,2048]{1,0:T(8,128)(2,1)S(1)}, u32[]{:S(2)}, u32[]{:S(2)}) collective-permute-start(bf16[256,2048]{1,0:T(8,128)(2,1)} %back_block.4), channel_id=1, source_target_pairs={{5,6},{6,5},{13,14},{14,13},{21,22},{22,21},{29,30},{30,29}} | collective-permute-start | bytes 3145736 | tf_op jit(solution)/shard_map/ppermute | solution.py:173
  135.8 41.1 %collective-permute-start.26 = (bf16[256,2048]{1,0:T(8,128)(2,1)S(1)}, bf16[256,2048]{1,0:T(8,128)(2,1)S(1)}, u32[]{:S(2)}, u32[]{:S(2)}) collective-permute-start(bf16[256,2048]{1,0:T(8,128)(2,1)S(1)} %copy-done.3), channel_id=1, source_target_pairs={{0,24},{1,25},{2,26},{3,27},{8,16},{9,17},{10,18},{11,19},{16,8},{... | collective-permute-start | bytes 3145736 | tf_op jit(solution)/shard_map/ppermute | solution.py:180
  140.3 6.4 %collective-permute-start.18 = (f32[256]{0:T(256)S(1)}, f32[256]{0:T(256)S(1)}, u32[]{:S(2)}, u32[]{:S(2)}) collective-permute-start(f32[256]{0:T(256)S(1)} %add.52), channel_id=1, source_target_pairs={{0,2},{1,3},{2,0},{3,1},{8,10},{9,11},{10,8},{11,9},{16,18},{17,19... | collective-permute-start | bytes 3080 | tf_op jit(solution)/shard_map/ppermute | solution.py:173
  144.1 9.2 %collective-permute-start.24 = (bf16[256,2048]{1,0:T(8,128)(2,1)S(1)}, bf16[256,2048]{1,0:T(8,128)(2,1)S(1)}, u32[]{:S(2)}, u32[]{:S(2)}) collective-permute-start(bf16[256,2048]{1,0:T(8,128)(2,1)S(1)} %back_block.5), channel_id=1, source_target_pairs={{4,6},{7,5},{5,4},{6,7},{12,14},{15,13},{13,12},{14,15},{20,22},{2... | collective-permute-start | bytes 3145736 | tf_op jit(solution)/shard_map/ppermute | solution.py:173
  144.9 12.8 %collective-permute-start.25 = (bf16[256,2048]{1,0:T(8,128)(2,1)S(1)}, bf16[256,2048]{1,0:T(8,128)(2,1)S(1)}, u32[]{:S(2)}, u32[]{:S(2)}) collective-permute-start(bf16[256,2048]{1,0:T(8,128)(2,1)S(1)} %add_convert_fusion.1), channel_id=1, source_target_pairs={{6,4},{5,7},{4,5},{7,6},{14,12},{13,15},{12,13},{15,14},{22,20},{2... | collective-permute-start | bytes 3145736 | tf_op jit(solution)/shard_map/ppermute | solution.py:173
  148.2 28.7 %collective-permute-start.28 = (bf16[256,2048]{1,0:T(8,128)(2,1)S(1)}, bf16[256,2048]{1,0:T(8,128)(2,1)}, u32[]{:S(2)}, u32[]{:S(2)}) collective-permute-start(bf16[256,2048]{1,0:T(8,128)(2,1)S(1)} %multiply_convert_fusion.2), channel_id=1, source_target_pairs={{0,16},{1,17},{2,18},{3,19},{8,24},{9,25},{10,26},{11,27},{16,0},{... | collective-permute-start | bytes 3145736 | tf_op jit(solution)/shard_map/ppermute | solution.py:180
  150.4 26.5 %collective-permute-start.27 = (bf16[256,2048]{1,0:T(8,128)(2,1)S(1)}, bf16[256,2048]{1,0:T(8,128)(2,1)}, u32[]{:S(2)}, u32[]{:S(2)}) collective-permute-start(bf16[256,2048]{1,0:T(8,128)(2,1)S(1)} %multiply_convert_fusion.2), channel_id=1, source_target_pairs={{0,8},{1,9},{2,10},{3,11},{8,0},{9,1},{10,2},{11,3},{16,24},{17,25... | collective-permute-start | bytes 3145736 | tf_op jit(solution)/shard_map/ppermute | solution.py:180
  153.4 28.1 %copy-start.1 = (bf16[256,2048]{1,0:T(8,128)(2,1)S(1)}, bf16[256,2048]{1,0:T(8,128)(2,1)}, u32[]{:S(2)}) copy-start(bf16[256,2048]{1,0:T(8,128)(2,1)} %copy-done) | copy-start | bytes 3145732
  153.4 26.1 %collective-permute-start.40 = (bf16[256,2048]{1,0:T(8,128)(2,1)S(1)}, bf16[256,2048]{1,0:T(8,128)(2,1)S(1)}, u32[]{:S(2)}, u32[]{:S(2)}) collective-permute-start(bf16[256,2048]{1,0:T(8,128)(2,1)S(1)} %multiply_convert_fusion.2), channel_id=1, source_target_pairs={{0,24},{1,25},{2,26},{3,27},{8,16},{9,17},{10,18},{11,19},{16,8},{... | collective-permute-start | bytes 3145736 | tf_op jit(solution)/shard_map/ppermute | solution.py:180
  157.7 26.5 %collective-permute-start.37 = (bf16[256,2048]{1,0:T(8,128)(2,1)S(1)}, bf16[256,2048]{1,0:T(8,128)(2,1)S(1)}, u32[]{:S(2)}, u32[]{:S(2)}) collective-permute-start(bf16[256,2048]{1,0:T(8,128)(2,1)S(1)} %multiply_convert_fusion.2), channel_id=1, source_target_pairs={{0,4},{1,5},{2,6},{3,7},{8,12},{9,13},{10,14},{11,15},{16,20},{17,... | collective-permute-start | bytes 3145736 | tf_op jit(solution)/shard_map/ppermute | solution.py:173
  176.9 8.6 %collective-permute-start.29 = (bf16[256,2048]{1,0:T(8,128)(2,1)S(1)}, bf16[256,2048]{1,0:T(8,128)(2,1)S(1)}, u32[]{:S(2)}, u32[]{:S(2)}) collective-permute-start(bf16[256,2048]{1,0:T(8,128)(2,1)S(1)} %add_convert_fusion), channel_id=1, source_target_pairs={{4,0},{5,1},{6,2},{7,3},{12,8},{13,9},{14,10},{15,11},{20,16},{21,... | collective-permute-start | bytes 3145736 | tf_op jit(solution)/shard_map/ppermute | solution.py:173
  179.5 8.3 %collective-permute-start.41 = (bf16[256,2048]{1,0:T(8,128)(2,1)S(1)}, bf16[256,2048]{1,0:T(8,128)(2,1)S(1)}, u32[]{:S(2)}, u32[]{:S(2)}) collective-permute-start(bf16[256,2048]{1,0:T(8,128)(2,1)S(1)} %collective-permute-done.40), channel_id=1, source_target_pairs={{0,4},{1,5},{2,6},{3,7},{8,12},{9,13},{10,14},{11,15},{16,20},{17,... | collective-permute-start | bytes 3145736 | tf_op jit(solution)/shard_map/ppermute | solution.py:173
  181.4 7.8 %collective-permute-start.33 = (bf16[256,2048]{1,0:T(8,128)(2,1)S(1)}, bf16[256,2048]{1,0:T(8,128)(2,1)S(1)}, u32[]{:S(2)}, u32[]{:S(2)}) collective-permute-start(bf16[256,2048]{1,0:T(8,128)(2,1)S(1)} %copy-done.1), channel_id=1, source_target_pairs={{0,4},{1,5},{2,6},{3,7},{8,12},{9,13},{10,14},{11,15},{16,20},{17,... | collective-permute-start | bytes 3145736 | tf_op jit(solution)/shard_map/ppermute | solution.py:173
  182.8 7.8 %collective-permute-start.34 = (bf16[256,2048]{1,0:T(8,128)(2,1)}, bf16[256,2048]{1,0:T(8,128)(2,1)S(1)}, u32[]{:S(2)}, u32[]{:S(2)}) collective-permute-start(bf16[256,2048]{1,0:T(8,128)(2,1)} %collective-permute-done.21), channel_id=1, source_target_pairs={{0,4},{1,5},{2,6},{3,7},{8,12},{9,13},{10,14},{11,15},{16,20},{17,... | collective-permute-start | bytes 3145736 | tf_op jit(solution)/shard_map/ppermute | solution.py:173
  184.2 9.8 %collective-permute-start.35 = (bf16[256,2048]{1,0:T(8,128)(2,1)}, bf16[256,2048]{1,0:T(8,128)(2,1)S(1)}, u32[]{:S(2)}, u32[]{:S(2)}) collective-permute-start(bf16[256,2048]{1,0:T(8,128)(2,1)} %collective-permute-done.22), channel_id=1, source_target_pairs={{0,4},{1,5},{2,6},{3,7},{8,12},{9,13},{10,14},{11,15},{16,20},{17,... | collective-permute-start | bytes 3145736 | tf_op jit(solution)/shard_map/ppermute | solution.py:173
  185.5 11.1 %collective-permute-start.36 = (bf16[256,2048]{1,0:T(8,128)(2,1)S(1)}, bf16[256,2048]{1,0:T(8,128)(2,1)S(1)}, u32[]{:S(2)}, u32[]{:S(2)}) collective-permute-start(bf16[256,2048]{1,0:T(8,128)(2,1)S(1)} %collective-permute-done.26), channel_id=1, source_target_pairs={{0,4},{1,5},{2,6},{3,7},{8,12},{9,13},{10,14},{11,15},{16,20},{17,... | collective-permute-start | bytes 3145736 | tf_op jit(solution)/shard_map/ppermute | solution.py:173
  187.9 8.8 %copy-start.9 = (bf16[256,2048]{1,0:T(8,128)(2,1)}, bf16[256,2048]{1,0:T(8,128)(2,1)S(1)}, u32[]{:S(2)}) copy-start(bf16[256,2048]{1,0:T(8,128)(2,1)S(1)} %collective-permute-done.41) | copy-start | bytes 3145732
  187.9 12.1 %collective-permute-start.38 = (bf16[256,2048]{1,0:T(8,128)(2,1)}, bf16[256,2048]{1,0:T(8,128)(2,1)S(1)}, u32[]{:S(2)}, u32[]{:S(2)}) collective-permute-start(bf16[256,2048]{1,0:T(8,128)(2,1)} %collective-permute-done.27), channel_id=1, source_target_pairs={{0,4},{1,5},{2,6},{3,7},{8,12},{9,13},{10,14},{11,15},{16,20},{17,... | collective-permute-start | bytes 3145736 | tf_op jit(solution)/shard_map/ppermute | solution.py:173
  189.3 10.7 %copy-start.10 = (bf16[256,2048]{1,0:T(8,128)(2,1)}, bf16[256,2048]{1,0:T(8,128)(2,1)S(1)}, u32[]{:S(2)}) copy-start(bf16[256,2048]{1,0:T(8,128)(2,1)S(1)} %collective-permute-done.33) | copy-start | bytes 3145732
  189.3 10.7 %collective-permute-start.39 = (bf16[256,2048]{1,0:T(8,128)(2,1)}, bf16[256,2048]{1,0:T(8,128)(2,1)S(1)}, u32[]{:S(2)}, u32[]{:S(2)}) collective-permute-start(bf16[256,2048]{1,0:T(8,128)(2,1)} %collective-permute-done.28), channel_id=1, source_target_pairs={{0,4},{1,5},{2,6},{3,7},{8,12},{9,13},{10,14},{11,15},{16,20},{17,... | collective-permute-start | bytes 3145736 | tf_op jit(solution)/shard_map/ppermute | solution.py:173
  190.6 9.3 %copy-start.11 = (bf16[256,2048]{1,0:T(8,128)(2,1)}, bf16[256,2048]{1,0:T(8,128)(2,1)S(1)}, u32[]{:S(2)}) copy-start(bf16[256,2048]{1,0:T(8,128)(2,1)S(1)} %collective-permute-done.34) | copy-start | bytes 3145732
  190.6 17.8 %collective-permute-start.32 = (bf16[256,2048]{1,0:T(8,128)(2,1)S(1)}, bf16[256,2048]{1,0:T(8,128)(2,1)}, u32[]{:S(2)}, u32[]{:S(2)}) collective-permute-start(bf16[256,2048]{1,0:T(8,128)(2,1)S(1)} %multiply_convert_fusion), channel_id=1, source_target_pairs={{0,24},{1,25},{2,26},{3,27},{8,16},{9,17},{10,18},{11,19},{16,8},{... | collective-permute-start | bytes 3145736 | tf_op jit(solution)/shard_map/ppermute | solution.py:180
  194.0 25.6 %collective-permute-start.31 = (bf16[256,2048]{1,0:T(8,128)(2,1)S(1)}, bf16[256,2048]{1,0:T(8,128)(2,1)}, u32[]{:S(2)}, u32[]{:S(2)}) collective-permute-start(bf16[256,2048]{1,0:T(8,128)(2,1)S(1)} %multiply_convert_fusion), channel_id=1, source_target_pairs={{0,16},{1,17},{2,18},{3,19},{8,24},{9,25},{10,26},{11,27},{16,0},{... | collective-permute-start | bytes 3145736 | tf_op jit(solution)/shard_map/ppermute | solution.py:180
  196.7 22.9 %collective-permute-start.30 = (bf16[256,2048]{1,0:T(8,128)(2,1)S(1)}, bf16[256,2048]{1,0:T(8,128)(2,1)}, u32[]{:S(2)}, u32[]{:S(2)}) collective-permute-start(bf16[256,2048]{1,0:T(8,128)(2,1)S(1)} %multiply_convert_fusion), channel_id=1, source_target_pairs={{0,8},{1,9},{2,10},{3,11},{8,0},{9,1},{10,2},{11,3},{16,24},{17,25... | collective-permute-start | bytes 3145736 | tf_op jit(solution)/shard_map/ppermute | solution.py:180
  (11 other events, 40.2 us)

commit v2 on v1

--- a/solution.py
+++ b/solution.py
@@ -120,11 +120,14 @@
     )(*args, weight)
 
 
-def pick_blocks(blocks, core):
-    count = 4
+def pick_blocks(blocks, core, count=4):
 
     def kernel(*refs):
-        given, taken, sems = refs[:5], refs[5:9], refs[-1]
+        given, taken = refs[:5], refs[5 : 5 + count]
+        held, sems, out_sems = refs[5 + count :]
+
+        def leave(k):
+            return pltpu.make_async_copy(held.at[k], taken[k], out_sems.at[k])
 
         @pl.when(lax.axis_index("section") == core)
         def _():
@@ -138,17 +141,24 @@
 
                     @pl.when(slot == j)
                     def _():
-                        pltpu.make_async_copy(given[j], taken[k], sems.at[k]).start()
+                        pltpu.make_async_copy(given[j], held.at[k], sems.at[k]).start()
 
             for k in range(count):
-                pltpu.make_async_copy(given[0], taken[k], sems.at[k]).wait()
+                pltpu.make_async_copy(given[0], held.at[k], sems.at[k]).wait()
+                leave(k).start()
+            for k in range(count):
+                leave(k).wait()
 
     return pl.pallas_call(
         kernel,
         out_shape=[jax.ShapeDtypeStruct(blocks[0].shape, blocks[0].dtype)] * count,
         in_specs=[ANYWHERE] * 5,
-        out_specs=[IN_VMEM] * count,
-        scratch_shapes=[pltpu.SemaphoreType.DMA((count,))],
+        out_specs=[ANYWHERE] * count,
+        scratch_shapes=[
+            pltpu.VMEM((count, *blocks[0].shape), blocks[0].dtype),
+            pltpu.SemaphoreType.DMA((count,)),
+            pltpu.SemaphoreType.DMA((count,)),
+        ],
         compiler_params=PARAMS,
         cost_estimate=COST,
         name="pick_blocks",
@@ -189,8 +199,9 @@
 
     round_a = [(0, 2), (3, 1), (1, 0), (2, 3)]
     round_b = [(2, 0), (1, 3), (0, 1), (3, 2)]
-    ends_in, ends_out = [(1, 0), (2, 3)], [(0, 1), (3, 2)]
+    ends_in = [(1, 0), (2, 3)]
     middle = [(1, 2), (2, 1)]
+    opposite = [(i, i ^ 3) for i in range(4)]
     swap = [(m, m) for m in range(parts)]
     near = [(i, i ^ 1) for i in range(4)]
     far = [(i, i ^ 2) for i in range(4)]
@@ -256,11 +267,12 @@
         own, a = tie((own, a))
         mid = along(own, middle, 0, 0)
         x_got.append(across(x_cols[3], 3, 0, 0))
-        z1 = times(along(a, swap, 0, 1), "a", 1, z1)
-        z1 = times(along(b, swap, 0, 1), "b", 1, z1)
-        ends = [(0, 0), (3, 3)]
-        inside = [(1, 1), (2, 2)]
-        z1 = times(along(mid, inside, 0, 1), "c", 1, z1, along(passed, ends, 0, 1))
+        here_a, here_b = along(a, swap, 0, 1), along(b, swap, 0, 1)
+        z1 = times(here_a, "a", 1, z1)
+        z1 = times(here_b, "b", 1, z1)
+        here_mid = along(mid, [(1, 1), (2, 2)], 0, 1)
+        here_passed = along(passed, [(0, 0), (3, 3)], 0, 1)
+        z1 = times(here_mid, "c", 1, z1, here_passed)
         blocks = [y1, a, b, mid, passed]
     else:
         here = jnp.where(section == 1, along(y1, swap, 0, 1), y1)
@@ -268,68 +280,65 @@
         x_got = [x_cols[0]] + [across(x_cols[k], k, 0, 0) for k in range(1, roles)]
         z1, blocks = forward_all(here, 1)
 
-    blocks, x_got = tie((blocks, x_got))
     y_cols = columns_of(blocks)
+    if line:
+        y_own = pick_blocks([here, here_a, here_b, here_mid, here_passed], 1, 1)[0]
+        z1, y_own = tie((z1, y_own))
+    else:
+        y_own = y_cols[0]
     grad = (head_f[None, :] * silu_slope(z1)).astype(jnp.bfloat16)
     y2 = (here.astype(jnp.float32) + jax.nn.silu(z1)).astype(jnp.bfloat16)
     value = jnp.sum(y2.astype(jnp.float32) * head_f[None, :], axis=1)
 
-    value, y_cols = tie((value, y_cols))
-    y_got = [y_cols[0]] + [across(y_cols[k], k, 0, 0) for k in range(1, roles)]
+    y_cols, x_got = tie((y_cols, x_got))
+    def term(which, grad, out=jnp.bfloat16):
+        return block_matmul(grad, weight, which, 1, True, None, out)
+
+    if line:
+        c = term("c", grad)
+        grad, value, y_cols, c = tie((grad, value, y_cols, c))
+    y_got = [y_own] + [across(y_cols[k], k, 0, 1) for k in range(1, roles)]
     value = along(value, swap, 1, 0)
     grad_0 = along(grad, swap, 1, 0)
 
-    def term(which, grad, out=jnp.bfloat16):
-        return block_matmul(grad, weight, which, 1, True, None, out)
-
-    if line:
-        c = term("c", grad)
-        passed = along(c, ends_out, 1, 1)
-        mid = along(c, middle, 1, 1)
-        grad, value, c = tie((grad, value, c))
+    if line:
+        got_c = along(c, opposite, 1, 1)
         b = term("b", grad)
         got_b = along(b, round_a, 1, 1)
         grad, b, grad_0 = tie((grad, b, grad_0))
-        a = term("a", grad, jnp.float32)
-        a = (a + passed.astype(jnp.float32)).astype(jnp.bfloat16)
-        a, y_got[1], y_got[2] = tie((a, y_got[1], y_got[2]))
+        a = term("a", grad)
         got_a = along(a, round_b, 1, 1)
-        grad, a = tie((grad, a))
+        value = sum_parts(value, 0)
+        grad, a, got_c, value, y_got[1:3] = tie((grad, a, got_c, value, y_got[1:3]))
         own = term("own", grad, jnp.float32)
-        back = own + (mid.astype(jnp.float32) + got_b.astype(jnp.float32))
+        back = own + (got_c.astype(jnp.float32) + got_b.astype(jnp.float32))
         back = (back + got_a.astype(jnp.float32)).astype(jnp.bfloat16)
     else:
+        value = sum_parts(value, 0)
         whole = jnp.stack([term(j, grad) for j in range(parts)])
         whole = jnp.where(section == 1, whole, jnp.zeros_like(whole))
         back = lax.psum_scatter(whole, "mp", scatter_dimension=0)
 
-    value = sum_parts(value, 0)
     err = (value - goal) * keep
     dz1 = (err[:, None] * grad_0.astype(jnp.float32)).astype(jnp.bfloat16)
-    dz1_got = [dz1] + [across(dz1, k, 0, 0) for k in range(1, roles)]
-    back, y_got, dz1_got[1], dz1_got[2] = tie((back, y_got, dz1_got[1], dz1_got[2]))
+    dz1_got = [across(dz1, k, 0, 1) for k in (1, 2)]
+    back, y_got[1:], dz1_got = tie((back, y_got[1:], dz1_got))
     back = along(back, swap, 1, 0)
 
     dx1 = err[:, None] * (head_f[None, :] + back.astype(jnp.float32))
     dx1 = dx1.astype(jnp.bfloat16).astype(jnp.float32)
     dz0 = (dx1 * slope).astype(jnp.bfloat16)
+    dz0, dz1, err = tie((dz0, dz1, err))
+    dz1_got.append(across(dz1, 3, 0, 1))
+    err = along(err, swap, 0, 1)
+    dz1_got.insert(0, (err[:, None] * grad.astype(jnp.float32)).astype(jnp.bfloat16))
     dz0_got = [dz0] + [across(dz0, k, 0, 0) for k in range(1, roles)]
-    y_got = [along(t, swap, 0, 1) for t in y_got]
-    dz1_got = [along(t, swap, 0, 1) for t in dz1_got]
-
-    def weight_grad(lefts, rights):
-        left, right = jnp.concatenate(lefts, axis=0), jnp.concatenate(rights, axis=0)
-        return mm(left, right, ((0,), (0,))).astype(jnp.bfloat16)
-
-    grads = lax.cond(
-        section == 1,
-        lambda x, y, p, q: weight_grad(y, q),
-        lambda x, y, p, q: weight_grad(x, p),
-        x_got,
-        y_got,
-        dz0_got,
-        dz1_got,
-    )
+
+    def own_of(zeroth, first):
+        return jnp.concatenate([jnp.where(section == 1, f, z) for z, f in zip(zeroth, first)], axis=0)
+
+    left, right = own_of(x_got, y_got), own_of(dz0_got, dz1_got)
+    grads = mm(left, right, ((0,), (0,))).astype(jnp.bfloat16)
     return grads[None]
 
 

time: 236 us -> 234 us (level)
  starting transfers between devices: 102 us -> 92 us
  waiting for transfers between devices: 80.4 us -> 89 us
  local copies, waits for them, and re-layouts: 5.83 us -> 2.19 us
  other arithmetic: 7.97 us -> 10.7 us
    ppermute x30 -> x22, starting transfers between devices: 64.9 us -> 37.9 us  [along(): lax.ppermute(block, AXES, [(place(r, source, i), place(r, target, j)) for...]
    ppermute x12, starting transfers between devices: 37.5 us -> 54.1 us  [across(): lax.ppermute(block, AXES, [(place(r, source, m), place(r ^ flip, target,...]
    ppermute x12, waiting for transfers between devices: 39.5 us -> 44.6 us  [across(): lax.ppermute(block, AXES, [(place(r, source, m), place(r ^ flip, target,...]
    unnamed x34 -> x26, local copies, waits for them, and re-layouts: 5.51 us -> 1.87 us
    ppermute x30 -> x22, waiting for transfers between devices: 40.9 us -> 44.4 us  [along(): lax.ppermute(block, AXES, [(place(r, source, i), place(r, target, j)) for...]
  transfers between devices with their start and end apart: 42 -> 34, of which waited for: 15 -> 18; matrix products, arithmetic and copies ran while one was open for 3% -> 3% of each run, Pallas kernels for 9% -> 9%
where the time goes in v2:
time: 234 us; the launch traced here: 233 us
  starting transfers between devices  92 us (39%)
  waiting for transfers between devices  89 us (38%)
  Pallas kernels  27.4 us (12%)
  matrix products  11.2 us (5%)
  other arithmetic  10.7 us (5%)
    ppermute x12, starting transfers between devices, across(): lax.ppermute(block, AXES, [(place(r, source, m), place(r ^ flip, target,...  54.1 us
    ppermute x12, waiting for transfers between devices, across(): lax.ppermute(block, AXES, [(place(r, source, m), place(r ^ flip, target,...  44.6 us
    ppermute x22, waiting for transfers between devices, along(): lax.ppermute(block, AXES, [(place(r, source, i), place(r, target, j)) for...  44.4 us
    ppermute x22, starting transfers between devices, along(): lax.ppermute(block, AXES, [(place(r, source, i), place(r, target, j)) for...  37.9 us
    pallas_call x12, Pallas kernels, block_matmul(): pl.pallas_call(kernel, out_shape=jax.ShapeDtypeStruct((rows, width), out)...  23.2 us
    dot_general x1, matrix products, mm(): lax.dot_general(a, b, (dims, ((), ())), preferred_element_type=jnp.float32)  11.2 us
  transfers between devices with their start and end apart: 34, of which 18 were waited for; matrix products, arithmetic and copies ran while one was open for 3% of the time, Pallas kernels for 9%

profile of v2, /device:TPU:0, one launch (start us, length us, event | category | flops | bytes accessed | tf_op | source)
XLA Modules:
  0.0 233.1 jit_solution(16103458756904001601)
XLA Ops:
  0.0 5.9 %collective-permute-start = (bf16[256,2048]{1,0:T(8,128)(2,1)}, bf16[256,2048]{1,0:T(8,128)(2,1)S(1)}, u32[]{:S(2)}, u32[]{:S(2)}) collective-permute-start(bf16[256,2048]{1,0:T(8,128)(2,1)} %bitcast.refs_0_), channel_id=1, source_target_pairs={{0,2},{3,1},{1,0},{2,3},{8,10},{11,9},{9,8},{10,11},{16,18},{19,17... | collective-permute-start | bytes 3145736 | tf_op jit(solution)/shard_map/ppermute | solution.py:183
  5.9 6.0 %forward_block.8.refs_1_ = f32[256,2048]{1,0:T(8,128)S(1)} custom-call(bf16[256,2048]{1,0:T(8,128)(2,1)} %bitcast.refs_0_, bf16[4,2048,2048]{2,1,0:T(8,128)(2,1)} %bitcast.5), custom_call_target="tpu_custom_call" | custom-call | flops 1024 | bytes 1024 | tf_op jit(solution)/shard_map/forward_block/pallas_call | solution.py:105
  12.0 1.9 collective-permute-start.3
  13.9 4.7 %collective-permute-done.refs_0_.refs_1_ = bf16[256,2048]{1,0:T(8,128)(2,1)S(1)} collective-permute-done((bf16[256,2048]{1,0:T(8,128)(2,1)}, bf16[256,2048]{1,0:T(8,128)(2,1)S(1)}, u32[]{:S(2)}, u32[]{:S(2)}) %collective-permute-start) | collective-permute-done | bytes 1048608 | tf_op jit(solution)/shard_map/ppermute | solution.py:183
  20.6 4.6 %forward_block.9.refs_1_ = f32[256,2048]{1,0:T(8,128)S(1)} custom-call(bf16[256,2048]{1,0:T(8,128)(2,1)S(1)} %collective-permute-done.refs_0_.refs_1_, f32[256,2048]{1,0:T(8,128)S(1)} %forward_block.8.refs_1_, bf16[4,2048,2048]{2,1,0:T(8,128)(2,1)} %bitcast.6), custom_call_target="tpu_custom_call" | custom-call | flops 1024 | bytes 1024 | tf_op jit(solution)/shard_map/forward_block/pallas_call | solution.py:105
  25.2 6.4 %collective-permute-done.3.refs_0_.refs_2_ = bf16[256,2048]{1,0:T(8,128)(2,1)S(1)} collective-permute-done((bf16[256,2048]{1,0:T(8,128)(2,1)}, bf16[256,2048]{1,0:T(8,128)(2,1)S(1)}, u32[]{:S(2)}, u32[]{:S(2)}) %collective-permute-start.3) | collective-permute-done | bytes 1048608 | tf_op jit(solution)/shard_map/ppermute | solution.py:183
  31.6 4.5 %forward_block.10.refs_2_ = f32[256,2048]{1,0:T(8,128)S(1)} custom-call(bf16[256,2048]{1,0:T(8,128)(2,1)S(1)} %collective-permute-done.3.refs_0_.refs_2_, f32[256,2048]{1,0:T(8,128)S(1)} %forward_block.9.refs_1_, bf16[4,2048,2048]{2,1,0:T(8,128)(2,1)} %bitcast.7), custom_call_target="tpu_custom_call" | custom-call | flops 1024 | bytes 1024 | tf_op jit(solution)/shard_map/forward_block/pallas_call | solution.py:105
  36.2 6.6 %collective-permute-done.2.refs_1_.refs_4_ = bf16[256,2048]{1,0:T(8,128)(2,1)S(1)} collective-permute-done((bf16[256,2048]{1,0:T(8,128)(2,1)S(1)}, bf16[256,2048]{1,0:T(8,128)(2,1)S(1)}, u32[]{:S(2)}, u32[]{:S(2)}) %collective-permute-start.2) | collective-permute-done | bytes 1048608 | tf_op jit(solution)/shard_map/ppermute | solution.py:183
  42.7 4.6 %forward_block.11 = f32[256,2048]{1,0:T(8,128)S(1)} custom-call(bf16[256,2048]{1,0:T(8,128)(2,1)S(1)} %collective-permute-done.1.refs_0_.refs_3_, bf16[256,2048]{1,0:T(8,128)(2,1)S(1)} %collective-permute-done.2.refs_1_.refs_4_, f32[256,2048]{1,0:T(8,128)S(1)} %forward_block.10.refs_2_, bf16[4,2048,2048]{2,1,0:T(8,128)(2,1)} %bitcast.8), custom_call_target="tpu_custom_call" | custom-call | flops 1024 | bytes 1024 | tf_op jit(solution)/shard_map/forward_block/pallas_call | solution.py:105
  47.3 1.9 add_convert_fusion.2.refs_0_
  50.6 3.5 %collective-permute-start.5 = (bf16[256,2048]{1,0:T(8,128)(2,1)S(1)}, bf16[256,2048]{1,0:T(8,128)(2,1)S(1)}, u32[]{:S(2)}, u32[]{:S(2)}) collective-permute-start(bf16[256,2048]{1,0:T(8,128)(2,1)S(1)} %add_convert_fusion.2.refs_0_), channel_id=1, source_target_pairs={{0,2},{3,1},{1,0},{2,3},{8,10},{11,9},{9,8},{10,11},{16,18},{19,17... | collective-permute-start | bytes 3145736 | tf_op jit(solution)/shard_map/ppermute | solution.py:183
  54.2 1.6 pick_blocks.3
  55.8 3.4 %collective-permute-start.7 = (bf16[256,2048]{1,0:T(8,128)(2,1)S(1)}, bf16[256,2048]{1,0:T(8,128)(2,1)S(1)}, u32[]{:S(2)}, u32[]{:S(2)}) collective-permute-start(bf16[256,2048]{1,0:T(8,128)(2,1)S(1)} %get-tuple-element.62), channel_id=1, source_target_pairs={{0,8},{1,9},{2,10},{3,11},{8,0},{9,1},{10,2},{11,3},{16,24},{17,25... | collective-permute-start | bytes 3145736 | tf_op jit(solution)/shard_map/ppermute | solution.py:190
  59.2 3.5 %collective-permute-start.8 = (bf16[256,2048]{1,0:T(8,128)(2,1)S(1)}, bf16[256,2048]{1,0:T(8,128)(2,1)S(1)}, u32[]{:S(2)}, u32[]{:S(2)}) collective-permute-start(bf16[256,2048]{1,0:T(8,128)(2,1)S(1)} %get-tuple-element.63), channel_id=1, source_target_pairs={{0,16},{1,17},{2,18},{3,19},{8,24},{9,25},{10,26},{11,27},{16,0},{... | collective-permute-start | bytes 3145736 | tf_op jit(solution)/shard_map/ppermute | solution.py:190
  62.8 2.3 collective-permute-start.6
  65.1 2.2 collective-permute-done.5.refs_1_
  67.3 5.2 %collective-permute-done.7 = bf16[256,2048]{1,0:T(8,128)(2,1)S(1)} collective-permute-done((bf16[256,2048]{1,0:T(8,128)(2,1)S(1)}, bf16[256,2048]{1,0:T(8,128)(2,1)S(1)}, u32[]{:S(2)}, u32[]{:S(2)}) %collective-permute-start.7) | collective-permute-done | bytes 1048608 | tf_op jit(solution)/shard_map/ppermute | solution.py:190
  72.5 3.4 %collective-permute-done.8 = bf16[256,2048]{1,0:T(8,128)(2,1)S(1)} collective-permute-done((bf16[256,2048]{1,0:T(8,128)(2,1)S(1)}, bf16[256,2048]{1,0:T(8,128)(2,1)S(1)}, u32[]{:S(2)}, u32[]{:S(2)}) %collective-permute-start.8) | collective-permute-done | bytes 1048608 | tf_op jit(solution)/shard_map/ppermute | solution.py:190
  75.9 4.5 %collective-permute-done.6.refs_2_ = bf16[256,2048]{1,0:T(8,128)(2,1)S(1)} collective-permute-done((bf16[256,2048]{1,0:T(8,128)(2,1)S(1)}, bf16[256,2048]{1,0:T(8,128)(2,1)S(1)}, u32[]{:S(2)}, u32[]{:S(2)}) %collective-permute-start.6) | collective-permute-done | bytes 1048608 | tf_op jit(solution)/shard_map/ppermute | solution.py:183
  85.2 3.4 %collective-permute-start.15 = (bf16[256,2048]{1,0:T(8,128)(2,1)S(1)}, bf16[256,2048]{1,0:T(8,128)(2,1)S(1)}, u32[]{:S(2)}, u32[]{:S(2)}) collective-permute-start(bf16[256,2048]{1,0:T(8,128)(2,1)S(1)} %get-tuple-element.76), channel_id=1, source_target_pairs={{0,24},{1,25},{2,26},{3,27},{8,16},{9,17},{10,18},{11,19},{16,8},{... | collective-permute-start | bytes 3145736 | tf_op jit(solution)/shard_map/ppermute | solution.py:190
  89.4 8.5 %collective-permute-done.11.refs_4_ = bf16[256,2048]{1,0:T(8,128)(2,1)S(1)} collective-permute-done((bf16[256,2048]{1,0:T(8,128)(2,1)S(1)}, bf16[256,2048]{1,0:T(8,128)(2,1)S(1)}, u32[]{:S(2)}, u32[]{:S(2)}) %collective-permute-start.11) | collective-permute-done | bytes 1048608 | tf_op jit(solution)/shard_map/ppermute | solution.py:183
  99.2 2.5 %pick_blocks.5 = (bf16[256,2048]{1,0:T(8,128)(2,1)}, bf16[256,2048]{1,0:T(8,128)(2,1)}, bf16[256,2048]{1,0:T(8,128)(2,1)}, bf16[256,2048]{1,0:T(8,128)(2,1)}) custom-call(bf16[256,2048]{1,0:T(8,128)(2,1)S(1)} %add_convert_fusion.2.refs_0_, bf16[256,2048]{1,0:T(8,128)(2,1)S(1)} %collective-permute-done.5.refs_1_, ...), custom_call_target="tpu_custom_call" | custom-call | flops 1024 | bytes 1024 | tf_op jit(solution)/shard_map/pick_blocks/pallas_call | solution.py:152
  108.3 1.6 collective-permute-start.17
  109.9 13.3 %collective-permute-start.21 = (bf16[256,2048]{1,0:T(8,128)(2,1)}, bf16[256,2048]{1,0:T(8,128)(2,1)}, u32[]{:S(2)}, u32[]{:S(2)}) collective-permute-start(bf16[256,2048]{1,0:T(8,128)(2,1)} %get-tuple-element.86), channel_id=1, source_target_pairs={{0,12},{1,13},{2,14},{3,15},{8,4},{9,5},{10,6},{11,7},{16,28},{17,... | collective-permute-start | bytes 3145736 | tf_op jit(solution)/shard_map/ppermute | solution.py:190
  123.2 2.3 collective-permute-start.22
  126.9 1.7 collective-permute-done.18
  128.5 1.9 collective-permute-start.19
  130.5 3.5 %collective-permute-done.19 = f32[256]{0:T(256)S(1)} collective-permute-done((f32[256]{0:T(256)S(1)}, f32[256]{0:T(256)S(1)}, u32[]{:S(2)}, u32[]{:S(2)}) %collective-permute-start.19) | collective-permute-done | bytes 1056 | tf_op jit(solution)/shard_map/ppermute | solution.py:183
  134.0 1.9 collective-permute-start.20
  137.3 3.1 %collective-permute-done.20 = f32[256]{0:T(256)S(1)} collective-permute-done((f32[256]{0:T(256)S(1)}, f32[256]{0:T(256)S(1)}, u32[]{:S(2)}, u32[]{:S(2)}) %collective-permute-start.20) | collective-permute-done | bytes 1056 | tf_op jit(solution)/shard_map/ppermute | solution.py:183
  140.4 1.8 collective-permute-start.23
  142.2 2.3 collective-permute-start.25
  145.6 1.7 collective-permute-start.24
  147.3 2.4 %multiply_convert_fusion.3 = bf16[256,2048]{1,0:T(8,128)(2,1)} fusion(bf16[256,2048]{1,0:T(8,128)(2,1)} %collective-permute-done.16, f32[256]{0:T(256)S(1)} %subtract_select_fusion), kind=kLoop, calls=%fused_computation.18 | loop fusion | flops 1572864 | bytes 2098176 | tf_op jit(solution)/shard_map/convert_element_type | solution.py:323
  149.7 11.8 %collective-permute-start.26 = (bf16[256,2048]{1,0:T(8,128)(2,1)}, bf16[256,2048]{1,0:T(8,128)(2,1)}, u32[]{:S(2)}, u32[]{:S(2)}) collective-permute-start(bf16[256,2048]{1,0:T(8,128)(2,1)} %multiply_convert_fusion.3), channel_id=1, source_target_pairs={{0,12},{1,13},{2,14},{3,15},{8,4},{9,5},{10,6},{11,7},{16,28},{17,... | collective-permute-start | bytes 3145736 | tf_op jit(solution)/shard_map/ppermute | solution.py:190
  161.5 2.3 collective-permute-start.27
  164.0 2.6 %add_convert_fusion = bf16[256,2048]{1,0:T(8,128)(2,1)S(1)} fusion(bf16[256,2048]{1,0:T(8,128)(2,1)} %collective-permute-done.24, f32[256,2048]{1,0:T(8,128)S(1)} %back_block.7, bf16[256,2048]{1,0:T(8,128)(2,1)} %collective-permute-done.23, bf16[256,2048]{1,0:T(8,128)(2,1)} %collective-permute-done.17), kind=kLoop, calls=%fused_computation.19 | loop fusion | flops 3670016 | bytes 6291456 | tf_op jit(solution)/shard_map/convert_element_type | solution.py:315
  166.7 6.5 %collective-permute-done.26 = bf16[256,2048]{1,0:T(8,128)(2,1)} collective-permute-done((bf16[256,2048]{1,0:T(8,128)(2,1)}, bf16[256,2048]{1,0:T(8,128)(2,1)}, u32[]{:S(2)}, u32[]{:S(2)}) %collective-permute-start.26) | collective-permute-done | bytes 1048608 | tf_op jit(solution)/shard_map/ppermute | solution.py:190
  173.2 2.3 collective-permute-done.27
  177.3 3.4 %collective-permute-done.28 = bf16[256,2048]{1,0:T(8,128)(2,1)S(1)} collective-permute-done((bf16[256,2048]{1,0:T(8,128)(2,1)S(1)}, bf16[256,2048]{1,0:T(8,128)(2,1)S(1)}, u32[]{:S(2)}, u32[]{:S(2)}) %collective-permute-start.28) | collective-permute-done | bytes 1048608 | tf_op jit(solution)/shard_map/ppermute | solution.py:183
  181.6 2.5 %collective-permute-start.32 = (bf16[256,2048]{1,0:T(8,128)(2,1)}, bf16[256,2048]{1,0:T(8,128)(2,1)S(1)}, u32[]{:S(2)}, u32[]{:S(2)}) collective-permute-start(bf16[256,2048]{1,0:T(8,128)(2,1)} %multiply_convert_fusion.3), channel_id=1, source_target_pairs={{0,28},{1,29},{2,30},{3,31},{8,20},{9,21},{10,22},{11,23},{16,12},... | collective-permute-start | bytes 3145736 | tf_op jit(solution)/shard_map/ppermute | solution.py:190
  184.1 4.1 %collective-permute-start.33 = (bf16[256,2048]{1,0:T(8,128)(2,1)S(1)}, bf16[256,2048]{1,0:T(8,128)(2,1)S(1)}, u32[]{:S(2)}, u32[]{:S(2)}) collective-permute-start(bf16[256,2048]{1,0:T(8,128)(2,1)S(1)} %multiply_convert_fusion.1), channel_id=1, source_target_pairs={{0,24},{1,25},{2,26},{3,27},{8,16},{9,17},{10,18},{11,19},{16,8},{... | collective-permute-start | bytes 3145736 | tf_op jit(solution)/shard_map/ppermute | solution.py:190
  189.6 2.8 %collective-permute-start.31 = (bf16[256,2048]{1,0:T(8,128)(2,1)S(1)}, bf16[256,2048]{1,0:T(8,128)(2,1)S(1)}, u32[]{:S(2)}, u32[]{:S(2)}) collective-permute-start(bf16[256,2048]{1,0:T(8,128)(2,1)S(1)} %multiply_convert_fusion.1), channel_id=1, source_target_pairs={{0,16},{1,17},{2,18},{3,19},{8,24},{9,25},{10,26},{11,27},{16,0},{... | collective-permute-start | bytes 3145736 | tf_op jit(solution)/shard_map/ppermute | solution.py:190
  192.4 2.4 %collective-permute-start.30 = (bf16[256,2048]{1,0:T(8,128)(2,1)S(1)}, bf16[256,2048]{1,0:T(8,128)(2,1)S(1)}, u32[]{:S(2)}, u32[]{:S(2)}) collective-permute-start(bf16[256,2048]{1,0:T(8,128)(2,1)S(1)} %multiply_convert_fusion.1), channel_id=1, source_target_pairs={{0,8},{1,9},{2,10},{3,11},{8,0},{9,1},{10,2},{11,3},{16,24},{17,25... | collective-permute-start | bytes 3145736 | tf_op jit(solution)/shard_map/ppermute | solution.py:190
  195.2 1.5 collective-permute-done.32
  196.7 13.8 %collective-permute-done.33 = bf16[256,2048]{1,0:T(8,128)(2,1)S(1)} collective-permute-done((bf16[256,2048]{1,0:T(8,128)(2,1)S(1)}, bf16[256,2048]{1,0:T(8,128)(2,1)S(1)}, u32[]{:S(2)}, u32[]{:S(2)}) %collective-permute-start.33) | collective-permute-done | bytes 1048608 | tf_op jit(solution)/shard_map/ppermute | solution.py:190
  210.6 11.0 %collective-permute-done.31 = bf16[256,2048]{1,0:T(8,128)(2,1)S(1)} collective-permute-done((bf16[256,2048]{1,0:T(8,128)(2,1)S(1)}, bf16[256,2048]{1,0:T(8,128)(2,1)S(1)}, u32[]{:S(2)}, u32[]{:S(2)}) %collective-permute-start.31) | collective-permute-done | bytes 1048608 | tf_op jit(solution)/shard_map/ppermute | solution.py:190
  221.9 11.2 %convert_bitcast_fusion = bf16[1,2048,2048]{2,1,0:T(8,128)(2,1)} fusion(bf16[256,2048]{1,0:T(8,128)(2,1)S(1)} %get-tuple-element.109, bf16[256,2048]{1,0:T(8,128)(2,1)S(1)} %get-tuple-element.110, bf16[256,2048]{1,0:T(8,128)(2,1)S(1)} %broadcast_select_fusion.5, bf16[256,2048]{1,0:T(8,128)(2,1)S(1)} %broadcast_select_fusion.6, ...), kind=kOutput, calls=%fused_computation | convolution fusion | flops 8627683328 | bytes 16777216 | tf_op jit(solution)/shard_map/dot_general | solution.py:29
  (86 shorter events, 25.5 us)
Async XLA Ops:
  0.0 18.6 %collective-permute-start = (bf16[256,2048]{1,0:T(8,128)(2,1)}, bf16[256,2048]{1,0:T(8,128)(2,1)S(1)}, u32[]{:S(2)}, u32[]{:S(2)}) collective-permute-start(bf16[256,2048]{1,0:T(8,128)(2,1)} %bitcast.refs_0_), channel_id=1, source_target_pairs={{0,2},{3,1},{1,0},{2,3},{8,10},{11,9},{9,8},{10,11},{16,18},{19,17... | collective-permute-start | bytes 3145736 | tf_op jit(solution)/shard_map/ppermute | solution.py:183
  12.0 19.6 %collective-permute-start.3 = (bf16[256,2048]{1,0:T(8,128)(2,1)}, bf16[256,2048]{1,0:T(8,128)(2,1)S(1)}, u32[]{:S(2)}, u32[]{:S(2)}) collective-permute-start(bf16[256,2048]{1,0:T(8,128)(2,1)} %bitcast.refs_0_), channel_id=1, source_target_pairs={{2,0},{1,3},{0,1},{3,2},{10,8},{9,11},{8,9},{11,10},{18,16},{17,19... | collective-permute-start | bytes 3145736 | tf_op jit(solution)/shard_map/ppermute | solution.py:183
  18.6 17.5 %collective-permute-start.1 = (bf16[256,2048]{1,0:T(8,128)(2,1)}, bf16[256,2048]{1,0:T(8,128)(2,1)S(1)}, u32[]{:S(2)}, u32[]{:S(2)}) collective-permute-start(bf16[256,2048]{1,0:T(8,128)(2,1)} %bitcast.refs_0_), channel_id=1, source_target_pairs={{1,2},{2,1},{9,10},{10,9},{17,18},{18,17},{25,26},{26,25}} | collective-permute-start | bytes 3145736 | tf_op jit(solution)/shard_map/ppermute | solution.py:183
  19.3 23.4 %collective-permute-start.2 = (bf16[256,2048]{1,0:T(8,128)(2,1)S(1)}, bf16[256,2048]{1,0:T(8,128)(2,1)S(1)}, u32[]{:S(2)}, u32[]{:S(2)}) collective-permute-start(bf16[256,2048]{1,0:T(8,128)(2,1)S(1)} %collective-permute-done.refs_0_.refs_1_), channel_id=1, source_target_pairs={{1,0},{2,3},{9,8},{10,11},{17,16},{18,19},{25,24},{26,27}} | collective-permute-start | bytes 3145736 | tf_op jit(solution)/shard_map/ppermute | solution.py:183
  49.3 13.5 %collective-permute-start.4 = (bf16[256,2048]{1,0:T(8,128)(2,1)S(1)}, bf16[256,2048]{1,0:T(8,128)(2,1)S(1)}, u32[]{:S(2)}, u32[]{:S(2)}) collective-permute-start(bf16[256,2048]{1,0:T(8,128)(2,1)S(1)} %add_convert_fusion.2.refs_0_), channel_id=1, source_target_pairs={{0,4},{1,5},{2,6},{3,7},{8,12},{9,13},{10,14},{11,15},{16,20},{17,... | collective-permute-start | bytes 3145736 | tf_op jit(solution)/shard_map/ppermute | solution.py:183
  50.6 16.7 %collective-permute-start.5 = (bf16[256,2048]{1,0:T(8,128)(2,1)S(1)}, bf16[256,2048]{1,0:T(8,128)(2,1)S(1)}, u32[]{:S(2)}, u32[]{:S(2)}) collective-permute-start(bf16[256,2048]{1,0:T(8,128)(2,1)S(1)} %add_convert_fusion.2.refs_0_), channel_id=1, source_target_pairs={{0,2},{3,1},{1,0},{2,3},{8,10},{11,9},{9,8},{10,11},{16,18},{19,17... | collective-permute-start | bytes 3145736 | tf_op jit(solution)/shard_map/ppermute | solution.py:183
  55.8 7.0 %copy-start.2 = (bf16[256,2048]{1,0:T(8,128)(2,1)}, bf16[256,2048]{1,0:T(8,128)(2,1)S(1)}, u32[]{:S(2)}) copy-start(bf16[256,2048]{1,0:T(8,128)(2,1)S(1)} %get-tuple-element.77) | copy-start | bytes 3145732
  55.8 16.7 %collective-permute-start.7 = (bf16[256,2048]{1,0:T(8,128)(2,1)S(1)}, bf16[256,2048]{1,0:T(8,128)(2,1)S(1)}, u32[]{:S(2)}, u32[]{:S(2)}) collective-permute-start(bf16[256,2048]{1,0:T(8,128)(2,1)S(1)} %get-tuple-element.62), channel_id=1, source_target_pairs={{0,8},{1,9},{2,10},{3,11},{8,0},{9,1},{10,2},{11,3},{16,24},{17,25... | collective-permute-start | bytes 3145736 | tf_op jit(solution)/shard_map/ppermute | solution.py:190
  59.2 40.0 %copy-start.10 = (bf16[2048]{0:T(1024)(128)(2,1)S(1)}, bf16[2048]{0:T(1024)(128)(2,1)}, u32[]{:S(2)}) copy-start(bf16[2048]{0:T(1024)(128)(2,1)} %param.7) | copy-start | bytes 12292
  59.2 16.7 %collective-permute-start.8 = (bf16[256,2048]{1,0:T(8,128)(2,1)S(1)}, bf16[256,2048]{1,0:T(8,128)(2,1)S(1)}, u32[]{:S(2)}, u32[]{:S(2)}) collective-permute-start(bf16[256,2048]{1,0:T(8,128)(2,1)S(1)} %get-tuple-element.63), channel_id=1, source_target_pairs={{0,16},{1,17},{2,18},{3,19},{8,24},{9,25},{10,26},{11,27},{16,0},{... | collective-permute-start | bytes 3145736 | tf_op jit(solution)/shard_map/ppermute | solution.py:190
  62.8 17.6 %collective-permute-start.6 = (bf16[256,2048]{1,0:T(8,128)(2,1)S(1)}, bf16[256,2048]{1,0:T(8,128)(2,1)S(1)}, u32[]{:S(2)}, u32[]{:S(2)}) collective-permute-start(bf16[256,2048]{1,0:T(8,128)(2,1)S(1)} %add_convert_fusion.2.refs_0_), channel_id=1, source_target_pairs={{2,0},{1,3},{0,1},{3,2},{10,8},{9,11},{8,9},{11,10},{18,16},{17,19... | collective-permute-start | bytes 3145736 | tf_op jit(solution)/shard_map/ppermute | solution.py:183
  72.5 29.2 %copy-start.8 = (bf16[256,2048]{1,0:T(8,128)(2,1)}, bf16[256,2048]{1,0:T(8,128)(2,1)S(1)}, u32[]{:S(2)}) copy-start(bf16[256,2048]{1,0:T(8,128)(2,1)S(1)} %collective-permute-done.7) | copy-start | bytes 3145732
  75.9 13.4 %copy-start.4 = (bf16[256,2048]{1,0:T(8,128)(2,1)}, bf16[256,2048]{1,0:T(8,128)(2,1)S(1)}, u32[]{:S(2)}) copy-start(bf16[256,2048]{1,0:T(8,128)(2,1)S(1)} %collective-permute-done.8) | copy-start | bytes 3145732
  80.4 8.2 %collective-permute-start.9 = (bf16[256,2048]{1,0:T(8,128)(2,1)S(1)}, bf16[256,2048]{1,0:T(8,128)(2,1)S(1)}, u32[]{:S(2)}, u32[]{:S(2)}) collective-permute-start(bf16[256,2048]{1,0:T(8,128)(2,1)S(1)} %add_convert_fusion.2.refs_0_), channel_id=1, source_target_pairs={{1,2},{2,1},{9,10},{10,9},{17,18},{18,17},{25,26},{26,25}} | collective-permute-start | bytes 3145736 | tf_op jit(solution)/shard_map/ppermute | solution.py:183
  81.1 16.7 %collective-permute-start.11 = (bf16[256,2048]{1,0:T(8,128)(2,1)S(1)}, bf16[256,2048]{1,0:T(8,128)(2,1)S(1)}, u32[]{:S(2)}, u32[]{:S(2)}) collective-permute-start(bf16[256,2048]{1,0:T(8,128)(2,1)S(1)} %collective-permute-done.5.refs_1_), channel_id=1, source_target_pairs={{1,0},{2,3},{9,8},{10,11},{17,16},{18,19},{25,24},{26,27}} | collective-permute-start | bytes 3145736 | tf_op jit(solution)/shard_map/ppermute | solution.py:183
  82.4 19.3 %collective-permute-start.14 = (bf16[256,2048]{1,0:T(8,128)(2,1)S(1)}, bf16[256,2048]{1,0:T(8,128)(2,1)S(1)}, u32[]{:S(2)}, u32[]{:S(2)}) collective-permute-start(bf16[256,2048]{1,0:T(8,128)(2,1)S(1)} %collective-permute-done.5.refs_1_), channel_id=1, source_target_pairs={{0,4},{1,5},{2,6},{3,7},{8,12},{9,13},{10,14},{11,15},{16,20},{17,... | collective-permute-start | bytes 3145736 | tf_op jit(solution)/shard_map/ppermute | solution.py:183
  83.8 18.0 %collective-permute-start.13 = (bf16[256,2048]{1,0:T(8,128)(2,1)S(1)}, bf16[256,2048]{1,0:T(8,128)(2,1)S(1)}, u32[]{:S(2)}, u32[]{:S(2)}) collective-permute-start(bf16[256,2048]{1,0:T(8,128)(2,1)S(1)} %collective-permute-done.6.refs_2_), channel_id=1, source_target_pairs={{0,4},{1,5},{2,6},{3,7},{8,12},{9,13},{10,14},{11,15},{16,20},{17,... | collective-permute-start | bytes 3145736 | tf_op jit(solution)/shard_map/ppermute | solution.py:183
  85.2 17.6 %collective-permute-start.15 = (bf16[256,2048]{1,0:T(8,128)(2,1)S(1)}, bf16[256,2048]{1,0:T(8,128)(2,1)S(1)}, u32[]{:S(2)}, u32[]{:S(2)}) collective-permute-start(bf16[256,2048]{1,0:T(8,128)(2,1)S(1)} %get-tuple-element.76), channel_id=1, source_target_pairs={{0,24},{1,25},{2,26},{3,27},{8,16},{9,17},{10,18},{11,19},{16,8},{... | collective-permute-start | bytes 3145736 | tf_op jit(solution)/shard_map/ppermute | solution.py:190
  88.6 14.1 %collective-permute-start.10 = (bf16[256,2048]{1,0:T(8,128)(2,1)S(1)}, bf16[256,2048]{1,0:T(8,128)(2,1)S(1)}, u32[]{:S(2)}, u32[]{:S(2)}) collective-permute-start(bf16[256,2048]{1,0:T(8,128)(2,1)S(1)} %collective-permute-done.9.refs_3_), channel_id=1, source_target_pairs={{1,5},{2,6},{9,13},{10,14},{17,21},{18,22},{25,29},{26,30}} | collective-permute-start | bytes 3145736 | tf_op jit(solution)/shard_map/ppermute | solution.py:183
  97.8 4.9 %collective-permute-start.12 = (bf16[256,2048]{1,0:T(8,128)(2,1)S(1)}, bf16[256,2048]{1,0:T(8,128)(2,1)S(1)}, u32[]{:S(2)}, u32[]{:S(2)}) collective-permute-start(bf16[256,2048]{1,0:T(8,128)(2,1)S(1)} %collective-permute-done.11.refs_4_), channel_id=1, source_target_pairs={{0,4},{3,7},{8,12},{11,15},{16,20},{19,23},{24,28},{27,31}} | collective-permute-start | bytes 3145736 | tf_op jit(solution)/shard_map/ppermute | solution.py:183
  102.8 1.0 copy-start.6
  103.7 1.0 copy-start
  105.9 19.6 %copy-start.11 = (s32[4]{0:T(128)S(1)}, s32[4]{0:T(128)}, u32[]{:S(2)}) copy-start(s32[4]{0:T(128)} %param.8) | copy-start | bytes 52
  105.9 30.0 %copy-start.12 = (s32[4]{0:T(128)S(1)}, s32[4]{0:T(128)}, u32[]{:S(2)}) copy-start(s32[4]{0:T(128)} %param.9) | copy-start | bytes 52
  107.0 35.2 %collective-permute-start.16 = (bf16[256,2048]{1,0:T(8,128)(2,1)S(1)}, bf16[256,2048]{1,0:T(8,128)(2,1)}, u32[]{:S(2)}, u32[]{:S(2)}) collective-permute-start(bf16[256,2048]{1,0:T(8,128)(2,1)S(1)} %get-tuple-element.88.refs_0_), channel_id=1, source_target_pairs={{4,0},{5,1},{6,2},{7,3},{12,8},{13,9},{14,10},{15,11},{20,16},{21,... | collective-permute-start | bytes 3145736 | tf_op jit(solution)/shard_map/ppermute | solution.py:183
  108.3 37.3 %collective-permute-start.17 = (bf16[256,2048]{1,0:T(8,128)(2,1)}, bf16[256,2048]{1,0:T(8,128)(2,1)}, u32[]{:S(2)}, u32[]{:S(2)}) collective-permute-start(bf16[256,2048]{1,0:T(8,128)(2,1)} %back_block.4), channel_id=1, source_target_pairs={{4,7},{5,6},{6,5},{7,4},{12,15},{13,14},{14,13},{15,12},{20,23},{2... | collective-permute-start | bytes 3145736 | tf_op jit(solution)/shard_map/ppermute | solution.py:183
  109.9 37.4 %collective-permute-start.21 = (bf16[256,2048]{1,0:T(8,128)(2,1)}, bf16[256,2048]{1,0:T(8,128)(2,1)}, u32[]{:S(2)}, u32[]{:S(2)}) collective-permute-start(bf16[256,2048]{1,0:T(8,128)(2,1)} %get-tuple-element.86), channel_id=1, source_target_pairs={{0,12},{1,13},{2,14},{3,15},{8,4},{9,5},{10,6},{11,7},{16,28},{17,... | collective-permute-start | bytes 3145736 | tf_op jit(solution)/shard_map/ppermute | solution.py:190
  123.2 24.0 %collective-permute-start.22 = (bf16[256,2048]{1,0:T(8,128)(2,1)}, bf16[256,2048]{1,0:T(8,128)(2,1)}, u32[]{:S(2)}, u32[]{:S(2)}) collective-permute-start(bf16[256,2048]{1,0:T(8,128)(2,1)} %get-tuple-element.87), channel_id=1, source_target_pairs={{0,20},{1,21},{2,22},{3,23},{8,28},{9,29},{10,30},{11,31},{16,4},{... | collective-permute-start | bytes 3145736 | tf_op jit(solution)/shard_map/ppermute | solution.py:190
  125.5 3.0 %collective-permute-start.18 = (f32[256]{0:T(256)S(1)}, f32[256]{0:T(256)S(1)}, u32[]{:S(2)}, u32[]{:S(2)}) collective-permute-start(f32[256]{0:T(256)S(1)} %get-tuple-element.85), channel_id=1, source_target_pairs={{4,0},{5,1},{6,2},{7,3},{12,8},{13,9},{14,10},{15,11},{20,16},{21,... | collective-permute-start | bytes 3080 | tf_op jit(solution)/shard_map/ppermute | solution.py:183
  128.5 5.5 %collective-permute-start.19 = (f32[256]{0:T(256)S(1)}, f32[256]{0:T(256)S(1)}, u32[]{:S(2)}, u32[]{:S(2)}) collective-permute-start(f32[256]{0:T(256)S(1)} %collective-permute-done.18), channel_id=1, source_target_pairs={{0,1},{1,0},{2,3},{3,2},{8,9},{9,8},{10,11},{11,10},{16,17},{17,16... | collective-permute-start | bytes 3080 | tf_op jit(solution)/shard_map/ppermute | solution.py:183
  134.0 6.4 %collective-permute-start.20 = (f32[256]{0:T(256)S(1)}, f32[256]{0:T(256)S(1)}, u32[]{:S(2)}, u32[]{:S(2)}) collective-permute-start(f32[256]{0:T(256)S(1)} %add.49), channel_id=1, source_target_pairs={{0,2},{1,3},{2,0},{3,1},{8,10},{9,11},{10,8},{11,9},{16,18},{17,19... | collective-permute-start | bytes 3080 | tf_op jit(solution)/shard_map/ppermute | solution.py:183
  140.4 23.5 %collective-permute-start.23 = (bf16[256,2048]{1,0:T(8,128)(2,1)}, bf16[256,2048]{1,0:T(8,128)(2,1)}, u32[]{:S(2)}, u32[]{:S(2)}) collective-permute-start(bf16[256,2048]{1,0:T(8,128)(2,1)} %back_block.5), channel_id=1, source_target_pairs={{4,6},{7,5},{5,4},{6,7},{12,14},{15,13},{13,12},{14,15},{20,22},{2... | collective-permute-start | bytes 3145736 | tf_op jit(solution)/shard_map/ppermute | solution.py:183
  142.2 24.4 %collective-permute-start.25 = (bf16[256,2048]{1,0:T(8,128)(2,1)}, bf16[256,2048]{1,0:T(8,128)(2,1)}, u32[]{:S(2)}, u32[]{:S(2)}) collective-permute-start(bf16[256,2048]{1,0:T(8,128)(2,1)} %get-tuple-element.92), channel_id=1, source_target_pairs={{0,28},{1,29},{2,30},{3,31},{8,20},{9,21},{10,22},{11,23},{16,12},... | collective-permute-start | bytes 3145736 | tf_op jit(solution)/shard_map/ppermute | solution.py:190
  145.6 18.4 %collective-permute-start.24 = (bf16[256,2048]{1,0:T(8,128)(2,1)}, bf16[256,2048]{1,0:T(8,128)(2,1)}, u32[]{:S(2)}, u32[]{:S(2)}) collective-permute-start(bf16[256,2048]{1,0:T(8,128)(2,1)} %back_block.6), channel_id=1, source_target_pairs={{6,4},{5,7},{4,5},{7,6},{14,12},{13,15},{12,13},{15,14},{22,20},{2... | collective-permute-start | bytes 3145736 | tf_op jit(solution)/shard_map/ppermute | solution.py:183
  149.7 23.4 %collective-permute-start.26 = (bf16[256,2048]{1,0:T(8,128)(2,1)}, bf16[256,2048]{1,0:T(8,128)(2,1)}, u32[]{:S(2)}, u32[]{:S(2)}) collective-permute-start(bf16[256,2048]{1,0:T(8,128)(2,1)} %multiply_convert_fusion.3), channel_id=1, source_target_pairs={{0,12},{1,13},{2,14},{3,15},{8,4},{9,5},{10,6},{11,7},{16,28},{17,... | collective-permute-start | bytes 3145736 | tf_op jit(solution)/shard_map/ppermute | solution.py:190
  161.5 13.9 %collective-permute-start.27 = (bf16[256,2048]{1,0:T(8,128)(2,1)}, bf16[256,2048]{1,0:T(8,128)(2,1)}, u32[]{:S(2)}, u32[]{:S(2)}) collective-permute-start(bf16[256,2048]{1,0:T(8,128)(2,1)} %multiply_convert_fusion.3), channel_id=1, source_target_pairs={{0,20},{1,21},{2,22},{3,23},{8,28},{9,29},{10,30},{11,31},{16,4},{... | collective-permute-start | bytes 3145736 | tf_op jit(solution)/shard_map/ppermute | solution.py:190
  163.9 12.8 %copy-start.1 = (bf16[256,2048]{1,0:T(8,128)(2,1)S(1)}, bf16[256,2048]{1,0:T(8,128)(2,1)}, u32[]{:S(2)}) copy-start(bf16[256,2048]{1,0:T(8,128)(2,1)} %copy-done) | copy-start | bytes 3145732
  163.9 12.8 %copy-start.3 = (bf16[256,2048]{1,0:T(8,128)(2,1)S(1)}, bf16[256,2048]{1,0:T(8,128)(2,1)}, u32[]{:S(2)}) copy-start(bf16[256,2048]{1,0:T(8,128)(2,1)} %copy-done.2) | copy-start | bytes 3145732
  166.6 10.3 %copy-start.5 = (bf16[256,2048]{1,0:T(8,128)(2,1)S(1)}, bf16[256,2048]{1,0:T(8,128)(2,1)}, u32[]{:S(2)}) copy-start(bf16[256,2048]{1,0:T(8,128)(2,1)} %copy-done.4) | copy-start | bytes 3145732
  166.6 10.3 %copy-start.7 = (bf16[256,2048]{1,0:T(8,128)(2,1)S(1)}, bf16[256,2048]{1,0:T(8,128)(2,1)}, u32[]{:S(2)}) copy-start(bf16[256,2048]{1,0:T(8,128)(2,1)} %copy-done.6) | copy-start | bytes 3145732
  175.4 5.3 %collective-permute-start.28 = (bf16[256,2048]{1,0:T(8,128)(2,1)S(1)}, bf16[256,2048]{1,0:T(8,128)(2,1)S(1)}, u32[]{:S(2)}, u32[]{:S(2)}) collective-permute-start(bf16[256,2048]{1,0:T(8,128)(2,1)S(1)} %add_convert_fusion), channel_id=1, source_target_pairs={{4,0},{5,1},{6,2},{7,3},{12,8},{13,9},{14,10},{15,11},{20,16},{21,... | collective-permute-start | bytes 3145736 | tf_op jit(solution)/shard_map/ppermute | solution.py:183
  177.3 12.1 %copy-start.9 = (bf16[256,2048]{1,0:T(8,128)(2,1)S(1)}, bf16[256,2048]{1,0:T(8,128)(2,1)}, u32[]{:S(2)}) copy-start(bf16[256,2048]{1,0:T(8,128)(2,1)} %copy-done.8) | copy-start | bytes 3145732
  181.6 15.1 %collective-permute-start.32 = (bf16[256,2048]{1,0:T(8,128)(2,1)}, bf16[256,2048]{1,0:T(8,128)(2,1)S(1)}, u32[]{:S(2)}, u32[]{:S(2)}) collective-permute-start(bf16[256,2048]{1,0:T(8,128)(2,1)} %multiply_convert_fusion.3), channel_id=1, source_target_pairs={{0,28},{1,29},{2,30},{3,31},{8,20},{9,21},{10,22},{11,23},{16,12},... | collective-permute-start | bytes 3145736 | tf_op jit(solution)/shard_map/ppermute | solution.py:190
  184.1 26.4 %collective-permute-start.33 = (bf16[256,2048]{1,0:T(8,128)(2,1)S(1)}, bf16[256,2048]{1,0:T(8,128)(2,1)S(1)}, u32[]{:S(2)}, u32[]{:S(2)}) collective-permute-start(bf16[256,2048]{1,0:T(8,128)(2,1)S(1)} %multiply_convert_fusion.1), channel_id=1, source_target_pairs={{0,24},{1,25},{2,26},{3,27},{8,16},{9,17},{10,18},{11,19},{16,8},{... | collective-permute-start | bytes 3145736 | tf_op jit(solution)/shard_map/ppermute | solution.py:190
  188.2 6.6 %collective-permute-start.29 = (f32[256]{0:T(256)S(1)}, f32[256]{0:T(256)S(1)}, u32[]{:S(2)}, u32[]{:S(2)}) collective-permute-start(f32[256]{0:T(256)S(1)} %subtract_select_fusion), channel_id=1, source_target_pairs={{0,4},{1,5},{2,6},{3,7},{8,12},{9,13},{10,14},{11,15},{16,20},{17,... | collective-permute-start | bytes 3080 | tf_op jit(solution)/shard_map/ppermute | solution.py:183
  189.6 32.0 %collective-permute-start.31 = (bf16[256,2048]{1,0:T(8,128)(2,1)S(1)}, bf16[256,2048]{1,0:T(8,128)(2,1)S(1)}, u32[]{:S(2)}, u32[]{:S(2)}) collective-permute-start(bf16[256,2048]{1,0:T(8,128)(2,1)S(1)} %multiply_convert_fusion.1), channel_id=1, source_target_pairs={{0,16},{1,17},{2,18},{3,19},{8,24},{9,25},{10,26},{11,27},{16,0},{... | collective-permute-start | bytes 3145736 | tf_op jit(solution)/shard_map/ppermute | solution.py:190
  192.4 29.4 %collective-permute-start.30 = (bf16[256,2048]{1,0:T(8,128)(2,1)S(1)}, bf16[256,2048]{1,0:T(8,128)(2,1)S(1)}, u32[]{:S(2)}, u32[]{:S(2)}) collective-permute-start(bf16[256,2048]{1,0:T(8,128)(2,1)S(1)} %multiply_convert_fusion.1), channel_id=1, source_target_pairs={{0,8},{1,9},{2,10},{3,11},{8,0},{9,1},{10,2},{11,3},{16,24},{17,25... | collective-permute-start | bytes 3145736 | tf_op jit(solution)/shard_map/ppermute | solution.py:190

commit v3 on v2

--- a/solution.py
+++ b/solution.py
@@ -29,7 +29,7 @@
     return lax.dot_general(a, b, (dims, ((), ())), preferred_element_type=jnp.float32)
 
 
-COST = pl.CostEstimate(flops=1024, bytes_accessed=1024, transcendentals=0)
+COST = pl.CostEstimate(flops=2 * 10**9, bytes_accessed=10**7, transcendentals=0)
 ANYWHERE = pl.BlockSpec(memory_space=pl.ANY)
 IN_VMEM = pl.BlockSpec(memory_space=pltpu.VMEM)
 PARAMS = pltpu.CompilerParams(vmem_limit_bytes=40 * 1024 * 1024)
@@ -55,7 +55,7 @@
     rows, depth = act.shape
     height, cols = weight.shape[1:]
     width = height if back else cols
-    tile = min(512, width)
+    tile = min(1024, width)
     tiles = width // tile
 
     def kernel(*refs):

time: 234 us -> 235 us (level)
  starting transfers between devices: 92 us -> 94.9 us
    ppermute x12, starting transfers between devices: 54.1 us -> 57.1 us  [across(): lax.ppermute(block, AXES, [(place(r, source, m), place(r ^ flip, target,...]
  transfers between devices with their start and end apart: 34 -> 34, of which waited for: 18 -> 17; matrix products, arithmetic and copies ran while one was open for 3% -> 3% of each run, Pallas kernels for 9% -> 9%
where the time goes in v3:
time: 235 us; the launch traced here: 234 us
  starting transfers between devices  94.9 us (40%)
  waiting for transfers between devices  87.5 us (37%)
  Pallas kernels  27.2 us (12%)
  matrix products  11.2 us (5%)
  other arithmetic  10.7 us (5%)
    ppermute x12, starting transfers between devices, across(): lax.ppermute(block, AXES, [(place(r, source, m), place(r ^ flip, target,...  57.1 us
    ppermute x22, waiting for transfers between devices, along(): lax.ppermute(block, AXES, [(place(r, source, i), place(r, target, j)) for...  44.8 us
    ppermute x12, waiting for transfers between devices, across(): lax.ppermute(block, AXES, [(place(r, source, m), place(r ^ flip, target,...  42.7 us
    ppermute x22, starting transfers between devices, along(): lax.ppermute(block, AXES, [(place(r, source, i), place(r, target, j)) for...  37.7 us
    pallas_call x12, Pallas kernels, block_matmul(): pl.pallas_call(kernel, out_shape=jax.ShapeDtypeStruct((rows, width), out)...  23.1 us
    dot_general x1, matrix products, mm(): lax.dot_general(a, b, (dims, ((), ())), preferred_element_type=jnp.float32)  11.2 us
  transfers between devices with their start and end apart: 34, of which 17 were waited for; matrix products, arithmetic and copies ran while one was open for 3% of the time, Pallas kernels for 9%

profile of v3, /device:TPU:0, one launch (start us, length us, event | category | flops | bytes accessed | tf_op | source)
XLA Modules:
  0.0 234.1 jit_solution(15393715610138403237)
XLA Ops:
  0.0 5.9 %collective-permute-start = (bf16[256,2048]{1,0:T(8,128)(2,1)}, bf16[256,2048]{1,0:T(8,128)(2,1)S(1)}, u32[]{:S(2)}, u32[]{:S(2)}) collective-permute-start(bf16[256,2048]{1,0:T(8,128)(2,1)} %bitcast.refs_0_), channel_id=1, source_target_pairs={{0,2},{3,1},{1,0},{2,3},{8,10},{11,9},{9,8},{10,11},{16,18},{19,17... | collective-permute-start | bytes 3145736 | tf_op jit(solution)/shard_map/ppermute | solution.py:183
  5.9 5.1 %forward_block.8.refs_1_ = f32[256,2048]{1,0:T(8,128)S(1)} custom-call(bf16[256,2048]{1,0:T(8,128)(2,1)} %bitcast.refs_0_, bf16[4,2048,2048]{2,1,0:T(8,128)(2,1)} %bitcast.5), custom_call_target="tpu_custom_call" | custom-call | flops 2000000000 | bytes 10000000 | tf_op jit(solution)/shard_map/forward_block/pallas_call | solution.py:105
  11.0 1.9 collective-permute-start.3
  12.9 5.7 %collective-permute-done.refs_0_.refs_1_ = bf16[256,2048]{1,0:T(8,128)(2,1)S(1)} collective-permute-done((bf16[256,2048]{1,0:T(8,128)(2,1)}, bf16[256,2048]{1,0:T(8,128)(2,1)S(1)}, u32[]{:S(2)}, u32[]{:S(2)}) %collective-permute-start) | collective-permute-done | bytes 1048608 | tf_op jit(solution)/shard_map/ppermute | solution.py:183
  20.6 4.8 %forward_block.9.refs_1_ = f32[256,2048]{1,0:T(8,128)S(1)} custom-call(bf16[256,2048]{1,0:T(8,128)(2,1)S(1)} %collective-permute-done.refs_0_.refs_1_, f32[256,2048]{1,0:T(8,128)S(1)} %forward_block.8.refs_1_, bf16[4,2048,2048]{2,1,0:T(8,128)(2,1)} %bitcast.6), custom_call_target="tpu_custom_call" | custom-call | flops 2000000000 | bytes 10000000 | tf_op jit(solution)/shard_map/forward_block/pallas_call | solution.py:105
  25.5 6.1 %collective-permute-done.3.refs_0_.refs_2_ = bf16[256,2048]{1,0:T(8,128)(2,1)S(1)} collective-permute-done((bf16[256,2048]{1,0:T(8,128)(2,1)}, bf16[256,2048]{1,0:T(8,128)(2,1)S(1)}, u32[]{:S(2)}, u32[]{:S(2)}) %collective-permute-start.3) | collective-permute-done | bytes 1048608 | tf_op jit(solution)/shard_map/ppermute | solution.py:183
  31.6 4.8 %forward_block.10.refs_2_ = f32[256,2048]{1,0:T(8,128)S(1)} custom-call(bf16[256,2048]{1,0:T(8,128)(2,1)S(1)} %collective-permute-done.3.refs_0_.refs_2_, f32[256,2048]{1,0:T(8,128)S(1)} %forward_block.9.refs_1_, bf16[4,2048,2048]{2,1,0:T(8,128)(2,1)} %bitcast.7), custom_call_target="tpu_custom_call" | custom-call | flops 2000000000 | bytes 10000000 | tf_op jit(solution)/shard_map/forward_block/pallas_call | solution.py:105
  36.4 6.3 %collective-permute-done.2.refs_1_.refs_4_ = bf16[256,2048]{1,0:T(8,128)(2,1)S(1)} collective-permute-done((bf16[256,2048]{1,0:T(8,128)(2,1)S(1)}, bf16[256,2048]{1,0:T(8,128)(2,1)S(1)}, u32[]{:S(2)}, u32[]{:S(2)}) %collective-permute-start.2) | collective-permute-done | bytes 1048608 | tf_op jit(solution)/shard_map/ppermute | solution.py:183
  42.7 4.9 %forward_block.11 = f32[256,2048]{1,0:T(8,128)S(1)} custom-call(bf16[256,2048]{1,0:T(8,128)(2,1)S(1)} %collective-permute-done.1.refs_0_.refs_3_, bf16[256,2048]{1,0:T(8,128)(2,1)S(1)} %collective-permute-done.2.refs_1_.refs_4_, f32[256,2048]{1,0:T(8,128)S(1)} %forward_block.10.refs_2_, bf16[4,2048,2048]{2,1,0:T(8,128)(2,1)} %bitcast.8), custom_call_target="tpu_custom_call" | custom-call | flops 2000000000 | bytes 10000000 | tf_op jit(solution)/shard_map/forward_block/pallas_call | solution.py:105
  47.6 1.9 add_convert_fusion.2.refs_0_
  49.5 1.4 collective-permute-start.4
  50.9 3.5 %collective-permute-start.5 = (bf16[256,2048]{1,0:T(8,128)(2,1)S(1)}, bf16[256,2048]{1,0:T(8,128)(2,1)S(1)}, u32[]{:S(2)}, u32[]{:S(2)}) collective-permute-start(bf16[256,2048]{1,0:T(8,128)(2,1)S(1)} %add_convert_fusion.2.refs_0_), channel_id=1, source_target_pairs={{0,2},{3,1},{1,0},{2,3},{8,10},{11,9},{9,8},{10,11},{16,18},{19,17... | collective-permute-start | bytes 3145736 | tf_op jit(solution)/shard_map/ppermute | solution.py:183
  54.4 1.6 pick_blocks.3
  56.1 3.4 %collective-permute-start.7 = (bf16[256,2048]{1,0:T(8,128)(2,1)S(1)}, bf16[256,2048]{1,0:T(8,128)(2,1)S(1)}, u32[]{:S(2)}, u32[]{:S(2)}) collective-permute-start(bf16[256,2048]{1,0:T(8,128)(2,1)S(1)} %get-tuple-element.62), channel_id=1, source_target_pairs={{0,8},{1,9},{2,10},{3,11},{8,0},{9,1},{10,2},{11,3},{16,24},{17,25... | collective-permute-start | bytes 3145736 | tf_op jit(solution)/shard_map/ppermute | solution.py:190
  59.5 3.5 %collective-permute-start.8 = (bf16[256,2048]{1,0:T(8,128)(2,1)S(1)}, bf16[256,2048]{1,0:T(8,128)(2,1)S(1)}, u32[]{:S(2)}, u32[]{:S(2)}) collective-permute-start(bf16[256,2048]{1,0:T(8,128)(2,1)S(1)} %get-tuple-element.63), channel_id=1, source_target_pairs={{0,16},{1,17},{2,18},{3,19},{8,24},{9,25},{10,26},{11,27},{16,0},{... | collective-permute-start | bytes 3145736 | tf_op jit(solution)/shard_map/ppermute | solution.py:190
  63.1 2.3 collective-permute-start.6
  65.4 2.2 collective-permute-done.5.refs_1_
  67.6 5.2 %collective-permute-done.7 = bf16[256,2048]{1,0:T(8,128)(2,1)S(1)} collective-permute-done((bf16[256,2048]{1,0:T(8,128)(2,1)S(1)}, bf16[256,2048]{1,0:T(8,128)(2,1)S(1)}, u32[]{:S(2)}, u32[]{:S(2)}) %collective-permute-start.7) | collective-permute-done | bytes 1048608 | tf_op jit(solution)/shard_map/ppermute | solution.py:190
  72.8 3.4 %collective-permute-done.8 = bf16[256,2048]{1,0:T(8,128)(2,1)S(1)} collective-permute-done((bf16[256,2048]{1,0:T(8,128)(2,1)S(1)}, bf16[256,2048]{1,0:T(8,128)(2,1)S(1)}, u32[]{:S(2)}, u32[]{:S(2)}) %collective-permute-start.8) | collective-permute-done | bytes 1048608 | tf_op jit(solution)/shard_map/ppermute | solution.py:190
  76.2 4.5 %collective-permute-done.6.refs_2_ = bf16[256,2048]{1,0:T(8,128)(2,1)S(1)} collective-permute-done((bf16[256,2048]{1,0:T(8,128)(2,1)S(1)}, bf16[256,2048]{1,0:T(8,128)(2,1)S(1)}, u32[]{:S(2)}, u32[]{:S(2)}) %collective-permute-start.6) | collective-permute-done | bytes 1048608 | tf_op jit(solution)/shard_map/ppermute | solution.py:183
  82.7 3.5 %collective-permute-start.15 = (bf16[256,2048]{1,0:T(8,128)(2,1)S(1)}, bf16[256,2048]{1,0:T(8,128)(2,1)S(1)}, u32[]{:S(2)}, u32[]{:S(2)}) collective-permute-start(bf16[256,2048]{1,0:T(8,128)(2,1)S(1)} %get-tuple-element.76), channel_id=1, source_target_pairs={{0,24},{1,25},{2,26},{3,27},{8,16},{9,17},{10,18},{11,19},{16,8},{... | collective-permute-start | bytes 3145736 | tf_op jit(solution)/shard_map/ppermute | solution.py:190
  89.6 8.4 %collective-permute-done.11.refs_4_ = bf16[256,2048]{1,0:T(8,128)(2,1)S(1)} collective-permute-done((bf16[256,2048]{1,0:T(8,128)(2,1)S(1)}, bf16[256,2048]{1,0:T(8,128)(2,1)S(1)}, u32[]{:S(2)}, u32[]{:S(2)}) %collective-permute-start.11) | collective-permute-done | bytes 1048608 | tf_op jit(solution)/shard_map/ppermute | solution.py:183
  99.5 2.5 %pick_blocks.5 = (bf16[256,2048]{1,0:T(8,128)(2,1)}, bf16[256,2048]{1,0:T(8,128)(2,1)}, bf16[256,2048]{1,0:T(8,128)(2,1)}, bf16[256,2048]{1,0:T(8,128)(2,1)}) custom-call(bf16[256,2048]{1,0:T(8,128)(2,1)S(1)} %add_convert_fusion.2.refs_0_, bf16[256,2048]{1,0:T(8,128)(2,1)S(1)} %collective-permute-done.5.refs_1_, ...), custom_call_target="tpu_custom_call" | custom-call | flops 2000000000 | bytes 10000000 | tf_op jit(solution)/shard_map/pick_blocks/pallas_call | solution.py:152
  107.6 1.6 collective-permute-start.17
  109.3 14.7 %collective-permute-start.21 = (bf16[256,2048]{1,0:T(8,128)(2,1)}, bf16[256,2048]{1,0:T(8,128)(2,1)}, u32[]{:S(2)}, u32[]{:S(2)}) collective-permute-start(bf16[256,2048]{1,0:T(8,128)(2,1)} %get-tuple-element.86), channel_id=1, source_target_pairs={{0,12},{1,13},{2,14},{3,15},{8,4},{9,5},{10,6},{11,7},{16,28},{17,... | collective-permute-start | bytes 3145736 | tf_op jit(solution)/shard_map/ppermute | solution.py:190
  124.0 2.3 collective-permute-start.22
  127.7 1.7 collective-permute-done.18
  129.3 1.9 collective-permute-start.19
  131.6 3.2 %collective-permute-done.19 = f32[256]{0:T(256)S(1)} collective-permute-done((f32[256]{0:T(256)S(1)}, f32[256]{0:T(256)S(1)}, u32[]{:S(2)}, u32[]{:S(2)}) %collective-permute-start.19) | collective-permute-done | bytes 1056 | tf_op jit(solution)/shard_map/ppermute | solution.py:183
  134.8 1.9 collective-permute-start.20
  137.7 3.5 %collective-permute-done.20 = f32[256]{0:T(256)S(1)} collective-permute-done((f32[256]{0:T(256)S(1)}, f32[256]{0:T(256)S(1)}, u32[]{:S(2)}, u32[]{:S(2)}) %collective-permute-start.20) | collective-permute-done | bytes 1056 | tf_op jit(solution)/shard_map/ppermute | solution.py:183
  141.2 1.6 collective-permute-start.23
  142.8 2.3 collective-permute-start.25
  146.2 1.7 collective-permute-start.24
  147.9 2.4 %multiply_convert_fusion.3 = bf16[256,2048]{1,0:T(8,128)(2,1)} fusion(bf16[256,2048]{1,0:T(8,128)(2,1)} %collective-permute-done.16, f32[256]{0:T(256)S(1)} %subtract_select_fusion), kind=kLoop, calls=%fused_computation.18 | loop fusion | flops 1572864 | bytes 2098176 | tf_op jit(solution)/shard_map/convert_element_type | solution.py:323
  150.3 12.5 %collective-permute-start.26 = (bf16[256,2048]{1,0:T(8,128)(2,1)}, bf16[256,2048]{1,0:T(8,128)(2,1)}, u32[]{:S(2)}, u32[]{:S(2)}) collective-permute-start(bf16[256,2048]{1,0:T(8,128)(2,1)} %multiply_convert_fusion.3), channel_id=1, source_target_pairs={{0,12},{1,13},{2,14},{3,15},{8,4},{9,5},{10,6},{11,7},{16,28},{17,... | collective-permute-start | bytes 3145736 | tf_op jit(solution)/shard_map/ppermute | solution.py:190
  162.8 2.3 collective-permute-start.27
  165.2 2.6 %add_convert_fusion = bf16[256,2048]{1,0:T(8,128)(2,1)S(1)} fusion(bf16[256,2048]{1,0:T(8,128)(2,1)} %collective-permute-done.24, f32[256,2048]{1,0:T(8,128)S(1)} %back_block.7, bf16[256,2048]{1,0:T(8,128)(2,1)} %collective-permute-done.23, bf16[256,2048]{1,0:T(8,128)(2,1)} %collective-permute-done.17), kind=kLoop, calls=%fused_computation.19 | loop fusion | flops 3670016 | bytes 6291456 | tf_op jit(solution)/shard_map/convert_element_type | solution.py:315
  167.9 6.5 %collective-permute-done.26 = bf16[256,2048]{1,0:T(8,128)(2,1)} collective-permute-done((bf16[256,2048]{1,0:T(8,128)(2,1)}, bf16[256,2048]{1,0:T(8,128)(2,1)}, u32[]{:S(2)}, u32[]{:S(2)}) %collective-permute-start.26) | collective-permute-done | bytes 1048608 | tf_op jit(solution)/shard_map/ppermute | solution.py:190
  174.4 2.3 collective-permute-done.27
  178.6 3.2 %collective-permute-done.28 = bf16[256,2048]{1,0:T(8,128)(2,1)S(1)} collective-permute-done((bf16[256,2048]{1,0:T(8,128)(2,1)S(1)}, bf16[256,2048]{1,0:T(8,128)(2,1)S(1)}, u32[]{:S(2)}, u32[]{:S(2)}) %collective-permute-start.28) | collective-permute-done | bytes 1048608 | tf_op jit(solution)/shard_map/ppermute | solution.py:183
  182.7 3.3 %collective-permute-start.32 = (bf16[256,2048]{1,0:T(8,128)(2,1)}, bf16[256,2048]{1,0:T(8,128)(2,1)S(1)}, u32[]{:S(2)}, u32[]{:S(2)}) collective-permute-start(bf16[256,2048]{1,0:T(8,128)(2,1)} %multiply_convert_fusion.3), channel_id=1, source_target_pairs={{0,28},{1,29},{2,30},{3,31},{8,20},{9,21},{10,22},{11,23},{16,12},... | collective-permute-start | bytes 3145736 | tf_op jit(solution)/shard_map/ppermute | solution.py:190
  186.0 3.3 %collective-permute-start.33 = (bf16[256,2048]{1,0:T(8,128)(2,1)S(1)}, bf16[256,2048]{1,0:T(8,128)(2,1)S(1)}, u32[]{:S(2)}, u32[]{:S(2)}) collective-permute-start(bf16[256,2048]{1,0:T(8,128)(2,1)S(1)} %multiply_convert_fusion.1), channel_id=1, source_target_pairs={{0,24},{1,25},{2,26},{3,27},{8,16},{9,17},{10,18},{11,19},{16,8},{... | collective-permute-start | bytes 3145736 | tf_op jit(solution)/shard_map/ppermute | solution.py:190
  190.7 2.8 %collective-permute-start.31 = (bf16[256,2048]{1,0:T(8,128)(2,1)S(1)}, bf16[256,2048]{1,0:T(8,128)(2,1)S(1)}, u32[]{:S(2)}, u32[]{:S(2)}) collective-permute-start(bf16[256,2048]{1,0:T(8,128)(2,1)S(1)} %multiply_convert_fusion.1), channel_id=1, source_target_pairs={{0,16},{1,17},{2,18},{3,19},{8,24},{9,25},{10,26},{11,27},{16,0},{... | collective-permute-start | bytes 3145736 | tf_op jit(solution)/shard_map/ppermute | solution.py:190
  193.4 3.4 %collective-permute-start.30 = (bf16[256,2048]{1,0:T(8,128)(2,1)S(1)}, bf16[256,2048]{1,0:T(8,128)(2,1)S(1)}, u32[]{:S(2)}, u32[]{:S(2)}) collective-permute-start(bf16[256,2048]{1,0:T(8,128)(2,1)S(1)} %multiply_convert_fusion.1), channel_id=1, source_target_pairs={{0,8},{1,9},{2,10},{3,11},{8,0},{9,1},{10,2},{11,3},{16,24},{17,25... | collective-permute-start | bytes 3145736 | tf_op jit(solution)/shard_map/ppermute | solution.py:190
  198.6 13.0 %collective-permute-done.33 = bf16[256,2048]{1,0:T(8,128)(2,1)S(1)} collective-permute-done((bf16[256,2048]{1,0:T(8,128)(2,1)S(1)}, bf16[256,2048]{1,0:T(8,128)(2,1)S(1)}, u32[]{:S(2)}, u32[]{:S(2)}) %collective-permute-start.33) | collective-permute-done | bytes 1048608 | tf_op jit(solution)/shard_map/ppermute | solution.py:190
  211.7 11.0 %collective-permute-done.31 = bf16[256,2048]{1,0:T(8,128)(2,1)S(1)} collective-permute-done((bf16[256,2048]{1,0:T(8,128)(2,1)S(1)}, bf16[256,2048]{1,0:T(8,128)(2,1)S(1)}, u32[]{:S(2)}, u32[]{:S(2)}) %collective-permute-start.31) | collective-permute-done | bytes 1048608 | tf_op jit(solution)/shard_map/ppermute | solution.py:190
  223.0 11.2 %convert_bitcast_fusion = bf16[1,2048,2048]{2,1,0:T(8,128)(2,1)} fusion(bf16[256,2048]{1,0:T(8,128)(2,1)S(1)} %get-tuple-element.109, bf16[256,2048]{1,0:T(8,128)(2,1)S(1)} %get-tuple-element.110, bf16[256,2048]{1,0:T(8,128)(2,1)S(1)} %broadcast_select_fusion.5, bf16[256,2048]{1,0:T(8,128)(2,1)S(1)} %broadcast_select_fusion.6, ...), kind=kOutput, calls=%fused_computation | convolution fusion | flops 8627683328 | bytes 16777216 | tf_op jit(solution)/shard_map/dot_general | solution.py:29
  (86 shorter events, 24.5 us)
Async XLA Ops:
  0.0 18.6 %collective-permute-start = (bf16[256,2048]{1,0:T(8,128)(2,1)}, bf16[256,2048]{1,0:T(8,128)(2,1)S(1)}, u32[]{:S(2)}, u32[]{:S(2)}) collective-permute-start(bf16[256,2048]{1,0:T(8,128)(2,1)} %bitcast.refs_0_), channel_id=1, source_target_pairs={{0,2},{3,1},{1,0},{2,3},{8,10},{11,9},{9,8},{10,11},{16,18},{19,17... | collective-permute-start | bytes 3145736 | tf_op jit(solution)/shard_map/ppermute | solution.py:183
  11.0 20.6 %collective-permute-start.3 = (bf16[256,2048]{1,0:T(8,128)(2,1)}, bf16[256,2048]{1,0:T(8,128)(2,1)S(1)}, u32[]{:S(2)}, u32[]{:S(2)}) collective-permute-start(bf16[256,2048]{1,0:T(8,128)(2,1)} %bitcast.refs_0_), channel_id=1, source_target_pairs={{2,0},{1,3},{0,1},{3,2},{10,8},{9,11},{8,9},{11,10},{18,16},{17,19... | collective-permute-start | bytes 3145736 | tf_op jit(solution)/shard_map/ppermute | solution.py:183
  18.6 17.8 %collective-permute-start.1 = (bf16[256,2048]{1,0:T(8,128)(2,1)}, bf16[256,2048]{1,0:T(8,128)(2,1)S(1)}, u32[]{:S(2)}, u32[]{:S(2)}) collective-permute-start(bf16[256,2048]{1,0:T(8,128)(2,1)} %bitcast.refs_0_), channel_id=1, source_target_pairs={{1,2},{2,1},{9,10},{10,9},{17,18},{18,17},{25,26},{26,25}} | collective-permute-start | bytes 3145736 | tf_op jit(solution)/shard_map/ppermute | solution.py:183
  19.3 23.4 %collective-permute-start.2 = (bf16[256,2048]{1,0:T(8,128)(2,1)S(1)}, bf16[256,2048]{1,0:T(8,128)(2,1)S(1)}, u32[]{:S(2)}, u32[]{:S(2)}) collective-permute-start(bf16[256,2048]{1,0:T(8,128)(2,1)S(1)} %collective-permute-done.refs_0_.refs_1_), channel_id=1, source_target_pairs={{1,0},{2,3},{9,8},{10,11},{17,16},{18,19},{25,24},{26,27}} | collective-permute-start | bytes 3145736 | tf_op jit(solution)/shard_map/ppermute | solution.py:183
  49.5 13.5 %collective-permute-start.4 = (bf16[256,2048]{1,0:T(8,128)(2,1)S(1)}, bf16[256,2048]{1,0:T(8,128)(2,1)S(1)}, u32[]{:S(2)}, u32[]{:S(2)}) collective-permute-start(bf16[256,2048]{1,0:T(8,128)(2,1)S(1)} %add_convert_fusion.2.refs_0_), channel_id=1, source_target_pairs={{0,4},{1,5},{2,6},{3,7},{8,12},{9,13},{10,14},{11,15},{16,20},{17,... | collective-permute-start | bytes 3145736 | tf_op jit(solution)/shard_map/ppermute | solution.py:183
  50.9 16.7 %collective-permute-start.5 = (bf16[256,2048]{1,0:T(8,128)(2,1)S(1)}, bf16[256,2048]{1,0:T(8,128)(2,1)S(1)}, u32[]{:S(2)}, u32[]{:S(2)}) collective-permute-start(bf16[256,2048]{1,0:T(8,128)(2,1)S(1)} %add_convert_fusion.2.refs_0_), channel_id=1, source_target_pairs={{0,2},{3,1},{1,0},{2,3},{8,10},{11,9},{9,8},{10,11},{16,18},{19,17... | collective-permute-start | bytes 3145736 | tf_op jit(solution)/shard_map/ppermute | solution.py:183
  56.1 7.0 %copy-start = (bf16[256,2048]{1,0:T(8,128)(2,1)}, bf16[256,2048]{1,0:T(8,128)(2,1)S(1)}, u32[]{:S(2)}) copy-start(bf16[256,2048]{1,0:T(8,128)(2,1)S(1)} %get-tuple-element.77) | copy-start | bytes 3145732
  56.1 16.7 %collective-permute-start.7 = (bf16[256,2048]{1,0:T(8,128)(2,1)S(1)}, bf16[256,2048]{1,0:T(8,128)(2,1)S(1)}, u32[]{:S(2)}, u32[]{:S(2)}) collective-permute-start(bf16[256,2048]{1,0:T(8,128)(2,1)S(1)} %get-tuple-element.62), channel_id=1, source_target_pairs={{0,8},{1,9},{2,10},{3,11},{8,0},{9,1},{10,2},{11,3},{16,24},{17,25... | collective-permute-start | bytes 3145736 | tf_op jit(solution)/shard_map/ppermute | solution.py:190
  59.5 39.9 %copy-start.10 = (bf16[2048]{0:T(1024)(128)(2,1)S(1)}, bf16[2048]{0:T(1024)(128)(2,1)}, u32[]{:S(2)}) copy-start(bf16[2048]{0:T(1024)(128)(2,1)} %param.7) | copy-start | bytes 12292
  59.5 16.7 %collective-permute-start.8 = (bf16[256,2048]{1,0:T(8,128)(2,1)S(1)}, bf16[256,2048]{1,0:T(8,128)(2,1)S(1)}, u32[]{:S(2)}, u32[]{:S(2)}) collective-permute-start(bf16[256,2048]{1,0:T(8,128)(2,1)S(1)} %get-tuple-element.63), channel_id=1, source_target_pairs={{0,16},{1,17},{2,18},{3,19},{8,24},{9,25},{10,26},{11,27},{16,0},{... | collective-permute-start | bytes 3145736 | tf_op jit(solution)/shard_map/ppermute | solution.py:190
  63.1 17.6 %collective-permute-start.6 = (bf16[256,2048]{1,0:T(8,128)(2,1)S(1)}, bf16[256,2048]{1,0:T(8,128)(2,1)S(1)}, u32[]{:S(2)}, u32[]{:S(2)}) collective-permute-start(bf16[256,2048]{1,0:T(8,128)(2,1)S(1)} %add_convert_fusion.2.refs_0_), channel_id=1, source_target_pairs={{2,0},{1,3},{0,1},{3,2},{10,8},{9,11},{8,9},{11,10},{18,16},{17,19... | collective-permute-start | bytes 3145736 | tf_op jit(solution)/shard_map/ppermute | solution.py:183
  72.8 29.3 %copy-start.8 = (bf16[256,2048]{1,0:T(8,128)(2,1)}, bf16[256,2048]{1,0:T(8,128)(2,1)S(1)}, u32[]{:S(2)}) copy-start(bf16[256,2048]{1,0:T(8,128)(2,1)S(1)} %collective-permute-done.7) | copy-start | bytes 3145732
  76.2 4.5 %copy-start.4 = (bf16[256,2048]{1,0:T(8,128)(2,1)}, bf16[256,2048]{1,0:T(8,128)(2,1)S(1)}, u32[]{:S(2)}) copy-start(bf16[256,2048]{1,0:T(8,128)(2,1)S(1)} %collective-permute-done.8) | copy-start | bytes 3145732
  80.7 8.2 %collective-permute-start.9 = (bf16[256,2048]{1,0:T(8,128)(2,1)S(1)}, bf16[256,2048]{1,0:T(8,128)(2,1)S(1)}, u32[]{:S(2)}, u32[]{:S(2)}) collective-permute-start(bf16[256,2048]{1,0:T(8,128)(2,1)S(1)} %add_convert_fusion.2.refs_0_), channel_id=1, source_target_pairs={{1,2},{2,1},{9,10},{10,9},{17,18},{18,17},{25,26},{26,25}} | collective-permute-start | bytes 3145736 | tf_op jit(solution)/shard_map/ppermute | solution.py:183
  81.4 16.7 %collective-permute-start.11 = (bf16[256,2048]{1,0:T(8,128)(2,1)S(1)}, bf16[256,2048]{1,0:T(8,128)(2,1)S(1)}, u32[]{:S(2)}, u32[]{:S(2)}) collective-permute-start(bf16[256,2048]{1,0:T(8,128)(2,1)S(1)} %collective-permute-done.5.refs_1_), channel_id=1, source_target_pairs={{1,0},{2,3},{9,8},{10,11},{17,16},{18,19},{25,24},{26,27}} | collective-permute-start | bytes 3145736 | tf_op jit(solution)/shard_map/ppermute | solution.py:183
  82.7 19.3 %collective-permute-start.15 = (bf16[256,2048]{1,0:T(8,128)(2,1)S(1)}, bf16[256,2048]{1,0:T(8,128)(2,1)S(1)}, u32[]{:S(2)}, u32[]{:S(2)}) collective-permute-start(bf16[256,2048]{1,0:T(8,128)(2,1)S(1)} %get-tuple-element.76), channel_id=1, source_target_pairs={{0,24},{1,25},{2,26},{3,27},{8,16},{9,17},{10,18},{11,19},{16,8},{... | collective-permute-start | bytes 3145736 | tf_op jit(solution)/shard_map/ppermute | solution.py:190
  86.2 15.8 %collective-permute-start.14 = (bf16[256,2048]{1,0:T(8,128)(2,1)S(1)}, bf16[256,2048]{1,0:T(8,128)(2,1)S(1)}, u32[]{:S(2)}, u32[]{:S(2)}) collective-permute-start(bf16[256,2048]{1,0:T(8,128)(2,1)S(1)} %collective-permute-done.5.refs_1_), channel_id=1, source_target_pairs={{0,4},{1,5},{2,6},{3,7},{8,12},{9,13},{10,14},{11,15},{16,20},{17,... | collective-permute-start | bytes 3145736 | tf_op jit(solution)/shard_map/ppermute | solution.py:183
  87.5 15.4 %collective-permute-start.13 = (bf16[256,2048]{1,0:T(8,128)(2,1)S(1)}, bf16[256,2048]{1,0:T(8,128)(2,1)S(1)}, u32[]{:S(2)}, u32[]{:S(2)}) collective-permute-start(bf16[256,2048]{1,0:T(8,128)(2,1)S(1)} %collective-permute-done.6.refs_2_), channel_id=1, source_target_pairs={{0,4},{1,5},{2,6},{3,7},{8,12},{9,13},{10,14},{11,15},{16,20},{17,... | collective-permute-start | bytes 3145736 | tf_op jit(solution)/shard_map/ppermute | solution.py:183
  88.9 14.1 %collective-permute-start.10 = (bf16[256,2048]{1,0:T(8,128)(2,1)S(1)}, bf16[256,2048]{1,0:T(8,128)(2,1)S(1)}, u32[]{:S(2)}, u32[]{:S(2)}) collective-permute-start(bf16[256,2048]{1,0:T(8,128)(2,1)S(1)} %collective-permute-done.9.refs_3_), channel_id=1, source_target_pairs={{1,5},{2,6},{9,13},{10,14},{17,21},{18,22},{25,29},{26,30}} | collective-permute-start | bytes 3145736 | tf_op jit(solution)/shard_map/ppermute | solution.py:183
  98.1 4.9 %collective-permute-start.12 = (bf16[256,2048]{1,0:T(8,128)(2,1)S(1)}, bf16[256,2048]{1,0:T(8,128)(2,1)S(1)}, u32[]{:S(2)}, u32[]{:S(2)}) collective-permute-start(bf16[256,2048]{1,0:T(8,128)(2,1)S(1)} %collective-permute-done.11.refs_4_), channel_id=1, source_target_pairs={{0,4},{3,7},{8,12},{11,15},{16,20},{19,23},{24,28},{27,31}} | collective-permute-start | bytes 3145736 | tf_op jit(solution)/shard_map/ppermute | solution.py:183
  102.0 1.0 copy-start.6
  103.1 1.0 copy-start.2
  105.2 21.0 %copy-start.11 = (s32[4]{0:T(128)S(1)}, s32[4]{0:T(128)}, u32[]{:S(2)}) copy-start(s32[4]{0:T(128)} %param.8) | copy-start | bytes 52
  105.3 26.0 %copy-start.12 = (s32[4]{0:T(128)S(1)}, s32[4]{0:T(128)}, u32[]{:S(2)}) copy-start(s32[4]{0:T(128)} %param.9) | copy-start | bytes 52
  106.3 36.5 %collective-permute-start.16 = (bf16[256,2048]{1,0:T(8,128)(2,1)S(1)}, bf16[256,2048]{1,0:T(8,128)(2,1)}, u32[]{:S(2)}, u32[]{:S(2)}) collective-permute-start(bf16[256,2048]{1,0:T(8,128)(2,1)S(1)} %get-tuple-element.88.refs_0_), channel_id=1, source_target_pairs={{4,0},{5,1},{6,2},{7,3},{12,8},{13,9},{14,10},{15,11},{20,16},{21,... | collective-permute-start | bytes 3145736 | tf_op jit(solution)/shard_map/ppermute | solution.py:183
  107.6 38.6 %collective-permute-start.17 = (bf16[256,2048]{1,0:T(8,128)(2,1)}, bf16[256,2048]{1,0:T(8,128)(2,1)}, u32[]{:S(2)}, u32[]{:S(2)}) collective-permute-start(bf16[256,2048]{1,0:T(8,128)(2,1)} %back_block.4), channel_id=1, source_target_pairs={{4,7},{5,6},{6,5},{7,4},{12,15},{13,14},{14,13},{15,12},{20,23},{2... | collective-permute-start | bytes 3145736 | tf_op jit(solution)/shard_map/ppermute | solution.py:183
  109.3 38.6 %collective-permute-start.21 = (bf16[256,2048]{1,0:T(8,128)(2,1)}, bf16[256,2048]{1,0:T(8,128)(2,1)}, u32[]{:S(2)}, u32[]{:S(2)}) collective-permute-start(bf16[256,2048]{1,0:T(8,128)(2,1)} %get-tuple-element.86), channel_id=1, source_target_pairs={{0,12},{1,13},{2,14},{3,15},{8,4},{9,5},{10,6},{11,7},{16,28},{17,... | collective-permute-start | bytes 3145736 | tf_op jit(solution)/shard_map/ppermute | solution.py:190
  124.0 23.9 %collective-permute-start.22 = (bf16[256,2048]{1,0:T(8,128)(2,1)}, bf16[256,2048]{1,0:T(8,128)(2,1)}, u32[]{:S(2)}, u32[]{:S(2)}) collective-permute-start(bf16[256,2048]{1,0:T(8,128)(2,1)} %get-tuple-element.87), channel_id=1, source_target_pairs={{0,20},{1,21},{2,22},{3,23},{8,28},{9,29},{10,30},{11,31},{16,4},{... | collective-permute-start | bytes 3145736 | tf_op jit(solution)/shard_map/ppermute | solution.py:190
  126.3 3.0 %collective-permute-start.18 = (f32[256]{0:T(256)S(1)}, f32[256]{0:T(256)S(1)}, u32[]{:S(2)}, u32[]{:S(2)}) collective-permute-start(f32[256]{0:T(256)S(1)} %get-tuple-element.85), channel_id=1, source_target_pairs={{4,0},{5,1},{6,2},{7,3},{12,8},{13,9},{14,10},{15,11},{20,16},{21,... | collective-permute-start | bytes 3080 | tf_op jit(solution)/shard_map/ppermute | solution.py:183
  129.3 5.5 %collective-permute-start.19 = (f32[256]{0:T(256)S(1)}, f32[256]{0:T(256)S(1)}, u32[]{:S(2)}, u32[]{:S(2)}) collective-permute-start(f32[256]{0:T(256)S(1)} %collective-permute-done.18), channel_id=1, source_target_pairs={{0,1},{1,0},{2,3},{3,2},{8,9},{9,8},{10,11},{11,10},{16,17},{17,16... | collective-permute-start | bytes 3080 | tf_op jit(solution)/shard_map/ppermute | solution.py:183
  134.8 6.4 %collective-permute-start.20 = (f32[256]{0:T(256)S(1)}, f32[256]{0:T(256)S(1)}, u32[]{:S(2)}, u32[]{:S(2)}) collective-permute-start(f32[256]{0:T(256)S(1)} %add.49), channel_id=1, source_target_pairs={{0,2},{1,3},{2,0},{3,1},{8,10},{9,11},{10,8},{11,9},{16,18},{17,19... | collective-permute-start | bytes 3080 | tf_op jit(solution)/shard_map/ppermute | solution.py:183
  141.2 24.0 %collective-permute-start.23 = (bf16[256,2048]{1,0:T(8,128)(2,1)}, bf16[256,2048]{1,0:T(8,128)(2,1)}, u32[]{:S(2)}, u32[]{:S(2)}) collective-permute-start(bf16[256,2048]{1,0:T(8,128)(2,1)} %back_block.5), channel_id=1, source_target_pairs={{4,6},{7,5},{5,4},{6,7},{12,14},{15,13},{13,12},{14,15},{20,22},{2... | collective-permute-start | bytes 3145736 | tf_op jit(solution)/shard_map/ppermute | solution.py:183
  142.8 25.0 %collective-permute-start.25 = (bf16[256,2048]{1,0:T(8,128)(2,1)}, bf16[256,2048]{1,0:T(8,128)(2,1)}, u32[]{:S(2)}, u32[]{:S(2)}) collective-permute-start(bf16[256,2048]{1,0:T(8,128)(2,1)} %get-tuple-element.92), channel_id=1, source_target_pairs={{0,28},{1,29},{2,30},{3,31},{8,20},{9,21},{10,22},{11,23},{16,12},... | collective-permute-start | bytes 3145736 | tf_op jit(solution)/shard_map/ppermute | solution.py:190
  146.2 19.0 %collective-permute-start.24 = (bf16[256,2048]{1,0:T(8,128)(2,1)}, bf16[256,2048]{1,0:T(8,128)(2,1)}, u32[]{:S(2)}, u32[]{:S(2)}) collective-permute-start(bf16[256,2048]{1,0:T(8,128)(2,1)} %back_block.6), channel_id=1, source_target_pairs={{6,4},{5,7},{4,5},{7,6},{14,12},{13,15},{12,13},{15,14},{22,20},{2... | collective-permute-start | bytes 3145736 | tf_op jit(solution)/shard_map/ppermute | solution.py:183
  150.3 24.1 %collective-permute-start.26 = (bf16[256,2048]{1,0:T(8,128)(2,1)}, bf16[256,2048]{1,0:T(8,128)(2,1)}, u32[]{:S(2)}, u32[]{:S(2)}) collective-permute-start(bf16[256,2048]{1,0:T(8,128)(2,1)} %multiply_convert_fusion.3), channel_id=1, source_target_pairs={{0,12},{1,13},{2,14},{3,15},{8,4},{9,5},{10,6},{11,7},{16,28},{17,... | collective-permute-start | bytes 3145736 | tf_op jit(solution)/shard_map/ppermute | solution.py:190
  162.8 13.9 %collective-permute-start.27 = (bf16[256,2048]{1,0:T(8,128)(2,1)}, bf16[256,2048]{1,0:T(8,128)(2,1)}, u32[]{:S(2)}, u32[]{:S(2)}) collective-permute-start(bf16[256,2048]{1,0:T(8,128)(2,1)} %multiply_convert_fusion.3), channel_id=1, source_target_pairs={{0,20},{1,21},{2,22},{3,23},{8,28},{9,29},{10,30},{11,31},{16,4},{... | collective-permute-start | bytes 3145736 | tf_op jit(solution)/shard_map/ppermute | solution.py:190
  165.2 12.8 %copy-start.1 = (bf16[256,2048]{1,0:T(8,128)(2,1)S(1)}, bf16[256,2048]{1,0:T(8,128)(2,1)}, u32[]{:S(2)}) copy-start(bf16[256,2048]{1,0:T(8,128)(2,1)} %copy-done) | copy-start | bytes 3145732
  165.2 12.8 %copy-start.3 = (bf16[256,2048]{1,0:T(8,128)(2,1)S(1)}, bf16[256,2048]{1,0:T(8,128)(2,1)}, u32[]{:S(2)}) copy-start(bf16[256,2048]{1,0:T(8,128)(2,1)} %copy-done.2) | copy-start | bytes 3145732
  167.8 10.3 %copy-start.5 = (bf16[256,2048]{1,0:T(8,128)(2,1)S(1)}, bf16[256,2048]{1,0:T(8,128)(2,1)}, u32[]{:S(2)}) copy-start(bf16[256,2048]{1,0:T(8,128)(2,1)} %copy-done.4) | copy-start | bytes 3145732
  167.9 10.3 %copy-start.7 = (bf16[256,2048]{1,0:T(8,128)(2,1)S(1)}, bf16[256,2048]{1,0:T(8,128)(2,1)}, u32[]{:S(2)}) copy-start(bf16[256,2048]{1,0:T(8,128)(2,1)} %copy-done.6) | copy-start | bytes 3145732
  176.7 5.1 %collective-permute-start.28 = (bf16[256,2048]{1,0:T(8,128)(2,1)S(1)}, bf16[256,2048]{1,0:T(8,128)(2,1)S(1)}, u32[]{:S(2)}, u32[]{:S(2)}) collective-permute-start(bf16[256,2048]{1,0:T(8,128)(2,1)S(1)} %add_convert_fusion), channel_id=1, source_target_pairs={{4,0},{5,1},{6,2},{7,3},{12,8},{13,9},{14,10},{15,11},{20,16},{21,... | collective-permute-start | bytes 3145736 | tf_op jit(solution)/shard_map/ppermute | solution.py:183
  178.6 12.0 %copy-start.9 = (bf16[256,2048]{1,0:T(8,128)(2,1)S(1)}, bf16[256,2048]{1,0:T(8,128)(2,1)}, u32[]{:S(2)}) copy-start(bf16[256,2048]{1,0:T(8,128)(2,1)} %copy-done.8) | copy-start | bytes 3145732
  182.7 15.9 %collective-permute-start.32 = (bf16[256,2048]{1,0:T(8,128)(2,1)}, bf16[256,2048]{1,0:T(8,128)(2,1)S(1)}, u32[]{:S(2)}, u32[]{:S(2)}) collective-permute-start(bf16[256,2048]{1,0:T(8,128)(2,1)} %multiply_convert_fusion.3), channel_id=1, source_target_pairs={{0,28},{1,29},{2,30},{3,31},{8,20},{9,21},{10,22},{11,23},{16,12},... | collective-permute-start | bytes 3145736 | tf_op jit(solution)/shard_map/ppermute | solution.py:190
  186.0 25.6 %collective-permute-start.33 = (bf16[256,2048]{1,0:T(8,128)(2,1)S(1)}, bf16[256,2048]{1,0:T(8,128)(2,1)S(1)}, u32[]{:S(2)}, u32[]{:S(2)}) collective-permute-start(bf16[256,2048]{1,0:T(8,128)(2,1)S(1)} %multiply_convert_fusion.1), channel_id=1, source_target_pairs={{0,24},{1,25},{2,26},{3,27},{8,16},{9,17},{10,18},{11,19},{16,8},{... | collective-permute-start | bytes 3145736 | tf_op jit(solution)/shard_map/ppermute | solution.py:190
  189.2 7.6 %collective-permute-start.29 = (f32[256]{0:T(256)S(1)}, f32[256]{0:T(256)S(1)}, u32[]{:S(2)}, u32[]{:S(2)}) collective-permute-start(f32[256]{0:T(256)S(1)} %subtract_select_fusion), channel_id=1, source_target_pairs={{0,4},{1,5},{2,6},{3,7},{8,12},{9,13},{10,14},{11,15},{16,20},{17,... | collective-permute-start | bytes 3080 | tf_op jit(solution)/shard_map/ppermute | solution.py:183
  190.7 32.0 %collective-permute-start.31 = (bf16[256,2048]{1,0:T(8,128)(2,1)S(1)}, bf16[256,2048]{1,0:T(8,128)(2,1)S(1)}, u32[]{:S(2)}, u32[]{:S(2)}) collective-permute-start(bf16[256,2048]{1,0:T(8,128)(2,1)S(1)} %multiply_convert_fusion.1), channel_id=1, source_target_pairs={{0,16},{1,17},{2,18},{3,19},{8,24},{9,25},{10,26},{11,27},{16,0},{... | collective-permute-start | bytes 3145736 | tf_op jit(solution)/shard_map/ppermute | solution.py:190
  193.4 29.4 %collective-permute-start.30 = (bf16[256,2048]{1,0:T(8,128)(2,1)S(1)}, bf16[256,2048]{1,0:T(8,128)(2,1)S(1)}, u32[]{:S(2)}, u32[]{:S(2)}) collective-permute-start(bf16[256,2048]{1,0:T(8,128)(2,1)S(1)} %multiply_convert_fusion.1), channel_id=1, source_target_pairs={{0,8},{1,9},{2,10},{3,11},{8,0},{9,1},{10,2},{11,3},{16,24},{17,25... | collective-permute-start | bytes 3145736 | tf_op jit(solution)/shard_map/ppermute | solution.py:190
